TPU v7x, 512 devices: a whole 4x8x8 slice. The times are simulated.
512 devices in a mesh: node: 64 (over y, z), cores: 8 (over x, core).
Axes of the slice: x: 4, y: 8, z: 8, core: 2. Of those that a mesh axis runs over, the one named last changes fastest.
Arguments:
- block_state: float32 [1024, 5, 4096], P(('node', 'cores')), as said below
- levels: int32 [1024], P(('node', 'cores')), may hold values from 0 to 3
- send_table: int32 [5, 25088], P(None, ('node', 'cores')), may hold values from 0 to 5, as said below
- receive_table: int32 [24576], P(('node', 'cores')), may hold values from 0 to 48, as said below
- migration: int32 [1024], P(('node', 'cores')), may hold values from 0 to 1023, as said below
- coarsen_flags: int32 [1024], P(('node', 'cores')), may hold values 0 or 1
Outputs:
- new_state: float32 [1024, 5, 4096], P(('node', 'cores'))
Inputs may be any that keep to these rules, and one draw needn't show every extreme that they name: `block_state`: densities lie between 0.86 and 1.17, every velocity component is at most 0.9 in magnitude, pressures are positive. `send_table`: Rows: block of the sending device (0 to 1), face (0 to 5), kind (0 same level, 1 sender coarser, 2 sender finer), first and second sub-window (0 to 3; below 2 for kind 0; 0 for kind 2). Entry k of a device is meant for the device k // 7 - 3 further along the curve, cyclically; entries no code names are unused. `receive_table`: the codes of one device are distinct; code c names the device c // 7 - 3 further along the curve, cyclically. On every device some curve offset uses all 7 positions. `migration`: A permutation of the blocks. Each position takes a block of its own device or of an adjacent device (index one lower or higher, no wrap), at most 1 from each neighbour; some device takes exactly 1 from its upper neighbour.
All inputs are finite; a program needn't handle non-finite values. No bound on the sum of `coarsen_flags` on one device may be relied on, other than what follows from the above.
Results may differ from a plain program's by a relative error of at most 0.0003.
Values sent between devices are 32-bit elements; how exact they have to be, the bound alone decides.
A program may use at most 64 MiB of HBM per device.

v0:
```python
import functools

import jax
import jax.numpy as jnp
import numpy as np
from jax import lax
from jax.experimental import pallas as pl
from jax.experimental.pallas import tpu as pltpu
from jax.sharding import PartitionSpec as P

MESH = pl.DeviceIdType.MESH
F32 = jnp.float32
BF16 = jnp.bfloat16
EDGE = 16
REACH = 3
CAP = 7
SLOTS = 49
VM = pl.BlockSpec(memory_space=pltpu.VMEM)
SM = pl.BlockSpec(memory_space=pltpu.SMEM)


def predict_table(n):
    w = np.zeros((2 * n, n))
    for c in range(n):
        w[2 * c, c] = 1.0
        if c == 0:
            w[1, 0:4] = np.array([5.0, 15.0, -5.0, 1.0]) / 16.0
        elif c == n - 2:
            w[2 * c + 1, n - 4 : n] = np.array([1.0, -5.0, 15.0, 5.0]) / 16.0
        elif c == n - 1:
            w[2 * c + 1, n - 1] = 1.0
        else:
            w[2 * c + 1, c - 1 : c + 3] = np.array([-1.0, 9.0, 9.0, -1.0]) / 16.0
    return w


def window_tables():
    depth = np.zeros((3, 3, 5))
    depth[0, :, 0:3] = np.eye(3)
    depth[1, :, 0:4] = predict_table(8)[0:3, 0:4]
    depth[2, 0, 0] = depth[2, 1, 2] = depth[2, 2, 4] = 1.0
    eye, fine = np.eye(16), predict_table(16)
    tangent = np.zeros((3, 4, 8, 16))
    for s in range(4):
        tangent[0, s] = eye[8 * (s % 2) : 8 * (s % 2) + 8]
        tangent[1, s] = fine[8 * s : 8 * s + 8]
        tangent[2, s] = eye[0::2]
    return depth, tangent


def constant_tables():
    depth, tangent = window_tables()
    pairs = [(0, s, 0) for s in range(2)]
    pairs += [(1, s, 2 * t) for s in range(4) for t in range(2)]
    pairs += [(2, 0, 0)]
    cols = []
    for kind, sa, sb in pairs:
        tile = np.zeros((16, 16, 8, 2, 8))
        for parity in range(2):
            tile[:, :, :, parity, :] = np.einsum(
                "pa,qb->abpq", tangent[kind, sa], tangent[kind, sb + parity]
            )
        cols.append(tile.reshape(256, 128))
    cols.append(np.zeros((256, 128)))
    tangents = np.concatenate(cols, 1)
    picks = np.zeros((2, 3, 2, 16, 10, 8))
    for kind in range(3):
        for b in range(2):
            for f in range(5):
                for i in range(3):
                    for layer in range(5):
                        picks[0, kind, b, f * 3 + i, b * 5 + f, layer] = depth[kind, i, layer]
                        picks[1, kind, b, f * 3 + i, b * 5 + f, 7 - layer] = depth[kind, i, layer]
    return tangents, picks.reshape(2, 96, 80)


def three_parts(x):
    high = x.astype(BF16)
    rest = x - high.astype(F32)
    middle = rest.astype(BF16)
    low = (rest - middle.astype(F32)).astype(BF16)
    return high, middle, low


def dot(a, b):
    return jnp.dot(a, b, preferred_element_type=F32)


def slab_kernel(x_ref, send_ref, level_ref, tan_ref, pick_ref, slab_ref, speed_ref, left, wide):
    fast = None
    for b in range(2):
        rho = x_ref[0, b * 5]
        inv = 1.0 / rho
        m = [x_ref[0, b * 5 + 1 + i] for i in range(3)]
        v = [mi * inv for mi in m]
        kinetic = m[0] * v[0] + m[1] * v[1] + m[2] * v[2]
        pressure = 0.4 * (x_ref[0, b * 5 + 4] - 0.5 * kinetic)
        speed = jnp.maximum(jnp.maximum(jnp.abs(v[0]), jnp.abs(v[1])), jnp.abs(v[2]))
        speed = speed + jnp.sqrt(1.4 * pressure * inv)
        top = jnp.max(speed)
        rated = top * lax.shift_left(jnp.int32(EDGE), level_ref[b]).astype(F32)
        fast = top if fast is None else jnp.maximum(fast, top)
        rate = rated if b == 0 else jnp.maximum(rate, rated)
    speed_ref[0:8] = jnp.full((8, 128), fast, F32)
    speed_ref[8:16] = jnp.full((8, 128), rate, F32)
    for g in range(6):
        side = g % 2
        planes = x_ref[g // 2, :, 8 * side : 8 * side + 8, :].reshape(80, 256)
        parts = three_parts(planes)
        rows = sum(dot(pick_ref[side], part) for part in parts)
        for n, part in enumerate(three_parts(rows)):
            for kind in range(3):
                left[kind, n, g * 32 : g * 32 + 32] = part[kind * 32 : kind * 32 + 32]
    for tile in range(6):
        kind = 0 if tile == 0 else 1 if tile < 5 else 2
        weights = tan_ref[:, tile * 256 : tile * 256 + 256]
        out = sum(dot(left[kind, n], weights) for n in range(3))
        wide[2 * tile] = out[:, 0:128].reshape(12, 16, 128)
        if tile < 5:
            wide[2 * tile + 1] = out[:, 128:256].reshape(12, 16, 128)
    lane = lax.broadcasted_iota(jnp.int32, (8, 128), 1)
    even = (lane & 8) == 0

    def entry(k, carry):
        blk, g, kind = send_ref[0, k], send_ref[1, k], send_ref[2, k]
        sa, sb = send_ref[3, k], send_ref[4, k]
        pair = jnp.where(kind == 0, sa % 2, jnp.where(kind == 1, 2 + sa * 2 + sb // 2, 10))
        parity = jnp.where(kind == 2, 0, sb % 2)
        low = wide[pair, g * 2 + blk, 0:8]
        high = wide[pair, g * 2 + blk, 8:16]
        first = jnp.where(even, low, pltpu.roll(high, 8, 1))
        second = jnp.where(even, pltpu.roll(low, 120, 1), high)
        slab_ref[k] = jnp.where(jnp.full((8, 128), parity, jnp.int32) == 0, first, second)
        return carry

    lax.fori_loop(0, SLOTS, entry, 0, unroll=7)


def exchange_kernel(
    nz, n_node, n_core,
    slab_ref, speed_ref, x_ref, recv_ref, mig_ref, level_ref,
    ghost_ref, moved_ref, top_ref,
    got, want_out, want_in, stage_g, stage_x, peak, peaks,
    slab_s, slab_r, want_s, want_r, move_s, move_r, peak_s, peak_r, own_s,
):
    node, core = lax.axis_index("node"), lax.axis_index("cores")
    me = node * n_core + core
    total = n_node * n_core
    ny = n_node // nz
    z, y = node % nz, node // nz

    def along(offset):
        other = (me + offset + total) % total
        return (other // n_core, other % n_core)

    groups = [
        [(node, (core + t) % n_core) for t in range(1, n_core)],
        [(y * nz + (z + t) % nz, core) for t in range(1, nz)],
        [(((y + t) % ny) * nz + z, core) for t in range(1, ny)],
    ]
    offsets = [o for o in range(-REACH, REACH + 1) if o != 0]
    partners = [d for group in groups for d in group] + [along(o) for o in offsets]
    barrier = pltpu.get_barrier_semaphore()
    for d in partners:
        pl.semaphore_signal(barrier, inc=1, device_id=d, device_id_type=MESH)
    peak[0] = speed_ref[...]
    wants = []
    for direction in (1, -1):
        want = jnp.int32(0)
        for j in range(2):
            source = mig_ref[j]
            want = want + jnp.where(source // 2 == me + direction, source % 2, 0)
        wants.append(want)
    for n in range(2):
        want_out[n] = jnp.full((8, 128), wants[n], jnp.int32).astype(F32)
    pl.semaphore_wait(barrier, len(partners))

    def send_peaks(phase):
        copies = []
        base = sum(len(g) for g in groups[:phase])
        for t, d in enumerate(groups[phase]):
            copies.append(
                pltpu.make_async_remote_copy(
                    src_ref=peak.at[phase],
                    dst_ref=peaks.at[base + t],
                    send_sem=peak_s.at[base + t],
                    recv_sem=peak_r.at[base + t],
                    device_id=d,
                    device_id_type=MESH,
                )
            )
        for c in copies:
            c.start()
        return copies

    def take_peaks(phase, copies):
        base = sum(len(g) for g in groups[:phase])
        for c in copies:
            c.wait_recv()
        best = peak[phase]
        for t in range(len(copies)):
            best = jnp.maximum(best, peaks[base + t])
        return best

    first = send_peaks(0)
    own = pltpu.make_async_copy(
        slab_ref.at[pl.ds(REACH * CAP, CAP)], got.at[pl.ds(REACH * CAP, CAP)], own_s
    )
    own.start()
    want_copies = []
    for n, direction in enumerate((1, -1)):
        want_copies.append(
            pltpu.make_async_remote_copy(
                src_ref=want_out.at[n],
                dst_ref=want_in.at[n],
                send_sem=want_s.at[n],
                recv_sem=want_r.at[n],
                device_id=along(direction),
                device_id_type=MESH,
            )
        )
    slab_copies = []
    for n, o in enumerate(offsets):
        slab_copies.append(
            pltpu.make_async_remote_copy(
                src_ref=slab_ref.at[pl.ds((o + REACH) * CAP, CAP)],
                dst_ref=got.at[pl.ds((REACH - o) * CAP, CAP)],
                send_sem=slab_s.at[n],
                recv_sem=slab_r.at[n],
                device_id=along(o),
                device_id_type=MESH,
            )
        )
    for c in want_copies + slab_copies:
        c.start()
    peak[1] = take_peaks(0, first)
    second = send_peaks(1)
    own.wait()
    for c in want_copies + slab_copies:
        c.wait_recv()
    lane = lax.broadcasted_iota(jnp.int32, (8, 128), 1)
    row = lax.broadcasted_iota(jnp.int32, (8, 128), 0)
    even = (lane & 8) == 0
    for b in range(2):
        scale = lax.shift_left(jnp.int32(EDGE), level_ref[b]).astype(F32)
        for g in range(6):
            for qa in range(2):
                at = (b * 6 + g) * 4 + 2 * qa
                left = got[recv_ref[at]]
                right = got[recv_ref[at + 1]]
                low = jnp.where(even, left, pltpu.roll(right, 8, 1))
                high = jnp.where(even, pltpu.roll(left, 120, 1), right)
                high = jnp.where(row == 7, scale, high)
                ghost_ref[b, g, qa, 0:8] = low
                ghost_ref[b, g, qa, 8:16] = high
    for n in range(2):
        second_block = want_in[n][0:1, 0:1] > 0.5
        stage_g[n] = jnp.where(second_block, ghost_ref[1], ghost_ref[0])
        for a in range(3):
            stage_x[n, a] = jnp.where(second_block, x_ref[a, 5:10], x_ref[a, 0:5])
    move_copies = []
    for n, direction in enumerate((-1, 1)):
        for m, (src, dst) in enumerate(
            (
                (stage_g.at[n], ghost_ref.at[3 - n]),
                (stage_x.at[n], moved_ref.at[1 - n]),
            )
        ):
            move_copies.append(
                pltpu.make_async_remote_copy(
                    src_ref=src,
                    dst_ref=dst,
                    send_sem=move_s.at[2 * n + m],
                    recv_sem=move_r.at[2 * n + m],
                    device_id=along(direction),
                    device_id_type=MESH,
                )
            )
    for c in move_copies:
        c.start()
    peak[2] = take_peaks(1, second)
    third = send_peaks(2)
    top_ref[...] = take_peaks(2, third)
    for c in move_copies:
        c.wait_recv()
    for c in first + second + third + want_copies + slab_copies + move_copies:
        c.wait_send()


def weno(values, centres, mirrored):
    half = 0.5 * (values[1:] - values[:-1])
    bend = half[1:] - half[:-1]
    rough = 1e-6 + (13.0 / 3.0) * (bend * bend)
    third = bend * (1.0 / 3.0)
    lo, n = centres, 9
    gl, gr = half[lo - 1 : lo - 1 + n], half[lo : lo + n]
    bl, bc, br = (slice(lo - 2 + t, lo - 2 + t + n) for t in range(3))
    tl = 2.0 * gl + bend[bl]
    tc = gl + gr
    tr = 2.0 * gr - bend[br]
    sl = rough[bl] + tl * tl
    sc = rough[bc] + tc * tc
    sr = rough[br] + tr * tr
    il = pl.reciprocal(sl, approx=True)
    ic = pl.reciprocal(sc, approx=True)
    ir = pl.reciprocal(sr, approx=True)
    wl, wc, wr = il * il, 6.0 * (ic * ic), ir * ir
    if mirrored:
        wl = 3.0 * wl
        cl = third[bl] + gl
        cc = third[bc] + gl
        cr = gr - 2.0 * third[br]
        total = wl * cl + wc * cc + wr * cr
        sign = -1.0
    else:
        wr = 3.0 * wr
        cl = gl + 2.0 * third[bl]
        cc = gr - third[bc]
        cr = gr - third[br]
        total = wl * cl + wc * cc + wr * cr
        sign = 1.0
    share = total * pl.reciprocal(wl + wc + wr, approx=True)
    centre = values[lo : lo + n]
    return centre + share if sign > 0 else centre - share


def update_kernel(
    x_ref, moved_ref, ghost_ref, top_ref, slot_ref, out_ref,
    cells, rims, plus, minus, change,
):
    rows = cells
    for b in range(2):
        slot = slot_ref[b]
        own = slot < 2
        for a in range(3):
            for f in range(5):
                base = (a * 5 + f) * 14 * 8
                mine = x_ref[a, jnp.minimum(slot, 1) * 5 + f]
                theirs = moved_ref[jnp.maximum(slot, 2) - 2, a, f]
                v = jnp.where(own, mine, theirs)
                for h in range(2):
                    low = v[0:8, h * 128 : h * 128 + 128]
                    high = v[8:16, h * 128 : h * 128 + 128]
                    r0, r1 = b * 2 + h, 4 + b * 2 + h
                    rows[pl.ds(base + 24 + r0, 8, stride=8), :] = low
                    rows[pl.ds(base + 88 + r0, 3, stride=8), :] = high[0:3]
                    rows[pl.ds(base + r1, 3, stride=8), :] = low[5:8]
                    rows[pl.ds(base + 24 + r1, 8, stride=8), :] = high
        for g in range(6):
            for h in range(2):
                base = (g // 2) * 128 + (g % 2) * 4 + b * 2 + h
                rims[pl.ds(base, 8, stride=8), :] = ghost_ref[slot, g, h, 0:8]
                rims[pl.ds(base + 64, 8, stride=8), :] = ghost_ref[slot, g, h, 8:16]
    for a in range(3):
        for f in range(5):
            base = (a * 5 + f) * 14 * 8
            for layer in range(3):
                rim = rims[pl.ds(a * 128 + (f * 3 + layer) * 8, 8), :]
                rows[pl.ds(base + (2 - layer) * 8, 4), :] = rim[0:4]
                rows[pl.ds(base + (11 + layer) * 8 + 4, 4), :] = rim[4:8]
    fastest = top_ref[0:8]
    step = 0.4 / top_ref[8:16]
    factor = step * rims[pl.ds(15 * 8, 8), :]
    for a in range(3):

        def flux(p, carry):
            u = [rows[pl.ds(pl.multiple_of(((a * 5 + f) * 14 + p) * 8, 8), 8), :] for f in range(5)]
            inv = 1.0 / u[0]
            v = [u[1 + i] * inv for i in range(3)]
            kinetic = u[1] * v[0] + u[2] * v[1] + u[3] * v[2]
            pressure = 0.4 * (u[4] - 0.5 * kinetic)
            flow = [u[1 + a]] + [u[1 + i] * v[a] for i in range(3)] + [(u[4] + pressure) * v[a]]
            flow[1 + a] = flow[1 + a] + pressure
            for f in range(5):
                plus[f, p] = 0.5 * (flow[f] + fastest * u[f])
                minus[f, p] = 0.5 * (flow[f] - fastest * u[f])
            return carry

        lax.fori_loop(0, 14, flux, 0, unroll=2)

        def field(f, carry):
            hat = weno(plus[f], 2, False) + weno(minus[f], 3, True)
            change[a, f] = factor * (hat[1:] - hat[:-1])
            return carry

        lax.fori_loop(0, 5, field, 0)
    for b in range(2):
        for a in range(3):
            for f in range(5):
                for half in range(2):
                    for h in range(2):
                        v = change[a, f, :, half * 4 + b * 2 + h, :]
                        if a == 0:
                            base = f * 14 * 8 + half * 4 + b * 2 + h
                            u = rows[pl.ds(base + 24, 8, stride=8), :]
                            v = u - v
                        out_ref[a, b * 5 + f, half * 8 : half * 8 + 8, h * 128 : h * 128 + 128] = v


def solution(mesh):
    n_node, n_core = mesh.shape["node"], mesh.shape["cores"]
    nz = max(1, int(round(n_node**0.5)))
    tangents, picks = constant_tables()
    smoother = predict_table(8) @ np.eye(16)[0::2]
    plane_smoother = np.kron(smoother, smoother)
    highest = lax.Precision.HIGHEST
    groups = n_core - 1 + nz - 1 + n_node // nz - 1

    def body(block_state, levels, send_table, receive_table, migration, coarsen_flags):
        cube = block_state.reshape(10, 16, 16, 16)
        x = jnp.stack(
            [
                cube.reshape(10, 16, 256),
                jnp.transpose(cube, (0, 2, 1, 3)).reshape(10, 16, 256),
                jnp.transpose(cube, (0, 3, 1, 2)).reshape(10, 16, 256),
            ]
        )
        slabs, speeds = pl.pallas_call(
            slab_kernel,
            out_shape=(
                jax.ShapeDtypeStruct((SLOTS, 8, 128), F32),
                jax.ShapeDtypeStruct((16, 128), F32),
            ),
            in_specs=[VM, SM, SM, VM, VM],
            out_specs=(VM, VM),
            scratch_shapes=[
                pltpu.VMEM((3, 3, 192, 256), BF16),
                pltpu.VMEM((11, 12, 16, 128), F32),
            ],
            compiler_params=pltpu.CompilerParams(vmem_limit_bytes=48 << 20),
            name="slabs",
        )(x, send_table, levels, jnp.asarray(tangents, BF16), jnp.asarray(picks, BF16))
        ghosts, moved, top = pl.pallas_call(
            functools.partial(exchange_kernel, nz, n_node, n_core),
            out_shape=(
                jax.ShapeDtypeStruct((4, 6, 2, 16, 128), F32),
                jax.ShapeDtypeStruct((2, 3, 5, 16, 256), F32),
                jax.ShapeDtypeStruct((16, 128), F32),
            ),
            in_specs=[VM, VM, VM, SM, SM, SM],
            out_specs=(VM, VM, VM),
            scratch_shapes=[
                pltpu.VMEM((SLOTS, 8, 128), F32),
                pltpu.VMEM((2, 8, 128), F32),
                pltpu.VMEM((2, 8, 128), F32),
                pltpu.VMEM((2, 6, 2, 16, 128), F32),
                pltpu.VMEM((2, 3, 5, 16, 256), F32),
                pltpu.VMEM((3, 16, 128), F32),
                pltpu.VMEM((groups, 16, 128), F32),
                pltpu.SemaphoreType.DMA((6,)),
                pltpu.SemaphoreType.DMA((6,)),
                pltpu.SemaphoreType.DMA((2,)),
                pltpu.SemaphoreType.DMA((2,)),
                pltpu.SemaphoreType.DMA((4,)),
                pltpu.SemaphoreType.DMA((4,)),
                pltpu.SemaphoreType.DMA((groups,)),
                pltpu.SemaphoreType.DMA((groups,)),
                pltpu.SemaphoreType.DMA,
            ],
            compiler_params=pltpu.CompilerParams(
                collective_id=0, has_side_effects=True, vmem_limit_bytes=48 << 20
            ),
            name="exchange",
        )(slabs, speeds, x, receive_table, migration, levels)
        me = lax.axis_index("node") * n_core + lax.axis_index("cores")
        source = migration // 2
        slot = jnp.where(source == me, migration % 2, jnp.where(source < me, 2, 3)).astype(jnp.int32)
        parts = pl.pallas_call(
            update_kernel,
            out_shape=jax.ShapeDtypeStruct((3, 10, 16, 256), F32),
            in_specs=[VM, VM, VM, VM, SM],
            out_specs=VM,
            scratch_shapes=[
                pltpu.VMEM((3 * 5 * 14 * 8, 128), F32),
                pltpu.VMEM((3 * 16 * 8, 128), F32),
                pltpu.VMEM((5, 14, 8, 128), F32),
                pltpu.VMEM((5, 14, 8, 128), F32),
                pltpu.VMEM((3, 5, 8, 8, 128), F32),
            ],
            compiler_params=pltpu.CompilerParams(vmem_limit_bytes=48 << 20),
            name="update",
        )(x, moved, ghosts, top, slot)
        second = jnp.transpose(parts[1].reshape(10, 16, 16, 16), (0, 2, 1, 3)).reshape(10, 16, 256)
        third = jnp.transpose(parts[2].reshape(10, 16, 16, 16), (0, 2, 3, 1)).reshape(10, 16, 256)
        migrated = parts[0] - second - third
        smooth = jnp.einsum(
            "nim,mt->nit", migrated, jnp.asarray(plane_smoother.T, F32), precision=highest
        )
        smooth = jnp.einsum("ia,nam->nim", jnp.asarray(smoother, F32), smooth, precision=highest)
        flagged = jnp.repeat(coarsen_flags == 1, 5)[:, None, None]
        result = jnp.where(flagged, smooth, migrated)
        return result.reshape(2, 5, 4096)

    both = ("node", "cores")
    return jax.shard_map(
        body,
        mesh=mesh,
        in_specs=(P(both, None, None), P(both), P(None, both), P(both), P(both), P(both)),
        out_specs=P(both, None, None),
        check_vma=False,
    )
```

profile of v0, /device:TPU:1, one launch (start us, length us, event | category | flops | bytes accessed | tf_op | source)
XLA Modules:
  0.0 48.5 jit_solution(17116384879459198531)
XLA Ops:
  0.0 1.0 %copy.16 = f32[2,5,4096]{2,1,0:T(8,128)S(1)} copy(f32[2,5,4096]{2,0,1:T(2,128)} %param.10) | data formatting | bytes 327680 | tf_op args[0]
  1.0 0.4 reshape.13
  1.5 0.4 copy.18
  1.9 0.6 %stack_reshape.6 = f32[1,10,16,256]{3,2,1,0:T(8,128)S(1)} reshape(f32[10,16,16,16]{3,2,1,0:T(8,128)S(1)} %copy.18) | data formatting | bytes 327680 | tf_op jit(solution)/shard_map/stack;reshape | solution.py:411
  2.4 0.0 copy-start
  2.4 0.0 copy-start.1
  2.5 0.0 copy-start.2
  2.5 0.0 copy-start.3
  2.5 0.4 copy.23
  2.8 0.0 copy-start.4
  2.8 0.0 copy-start.5
  2.8 0.1 stack_reshape_reshape.3
  3.0 0.6 %copy-done = bf16[256,1536]{1,0:T(8,128)(2,1)S(1)} copy-done((bf16[256,1536]{1,0:T(8,128)(2,1)S(1)}, bf16[256,1536]{1,0:T(8,128)(2,1)}, u32[]{:S(2)}) %copy-start) | copy-done | bytes 786456
  3.6 0.0 copy-done.1
  3.6 0.0 copy-done.2
  3.6 0.0 copy-done.3
  3.6 2.6 %slabs.1 = (f32[49,8,128]{2,1,0:T(8,128)S(1)}, f32[16,128]{1,0:T(8,128)S(1)}) custom-call(f32[3,10,16,256]{3,2,1,0:T(8,128)S(1)} %pad_maximum_fusion.x_ref, s32[5,49]{1,0:T(8,128)S(1)} %copy-done.2, s32[2]{0:T(128)S(1)} %copy-done.3, bf16[256,1536]{1,0:T(8,128)(2,1)S(1)} %copy-done, bf16[2,96,80]{2,1,0:T(8,128)(2,1)S(1)} %copy-done.1), custom_call_target="tpu_custom_call" | custom-call | tf_op jit(solution)/shard_map/slabs/pallas_call | solution.py:418
  6.2 0.0 copy-done.4
  6.2 0.0 copy-done.5
  6.2 29.7 %exchange.1 = (f32[4,6,2,16,128]{4,3,2,1,0:T(8,128)S(1)}, f32[2,3,5,16,256]{4,3,2,1,0:T(8,128)S(1)}, f32[16,128]{1,0:T(8,128)S(1)}) custom-call(f32[49,8,128]{2,1,0:T(8,128)S(1)} %get-tuple-element.10.slab_ref, f32[16,128]{1,0:T(8,128)S(1)} %get-tuple-element.11.speed_ref, f32[3,10,16,256]{3,2,1,0:T(8,128)S(1)} %pad_maximum_fusion.x_ref, s32[48]{0:T(128)S(1)} %copy-done.4, ...), custom_call_target="tpu_custom_call" | custom-call | tf_op jit(solution)/shard_map/exchange/pallas_call | solution.py:433
  35.9 3.4 %update.1 = f32[3,10,16,256]{3,2,1,0:T(8,128)S(1)} custom-call(f32[3,10,16,256]{3,2,1,0:T(8,128)S(1)} %pad_maximum_fusion.x_ref, f32[2,3,5,16,256]{4,3,2,1,0:T(8,128)S(1)} %get-tuple-element.12.moved_ref, f32[4,6,2,16,128]{4,3,2,1,0:T(8,128)S(1)} %get-tuple-element.13.ghost_ref, f32[16,128]{1,0:T(8,128)S(1)} %get-tuple-element.14.top_ref, ...), custom_call_target="tpu_custom_call" | custom-call | tf_op jit(solution)/shard_map/update/pallas_call | solution.py:468
  39.3 0.4 reshape_squeeze.6
  39.7 1.5 %copy.20 = f32[10,16,16,16]{3,2,1,0:T(8,128)} copy(f32[10,16,16,16]{3,1,2,0:T(8,128)S(1)} %bitcast.36) | data formatting | bytes 327680 | tf_op jit(solution)/shard_map/transpose | solution.py:483
  41.2 1.8 %reshape.14 = f32[10,16,256]{2,1,0:T(8,128)S(1)} reshape(f32[10,16,16,16]{3,2,1,0:T(8,128)} %copy.20) | data formatting | bytes 327680 | tf_op jit(solution)/shard_map/reshape | solution.py:483
  43.0 0.4 reshape_squeeze.7
  43.4 1.6 %copy.21 = f32[10,16,16,16]{3,2,1,0:T(8,128)} copy(f32[10,16,16,16]{2,1,3,0:T(8,128)S(1)} %bitcast.37) | data formatting | bytes 327680 | tf_op jit(solution)/shard_map/transpose | solution.py:484
  45.0 0.0 copy-start.6
  45.0 0.0 copy-start.8
  45.0 0.0 copy-start.7
  45.0 1.8 %reshape.15 = f32[10,16,256]{2,1,0:T(8,128)S(1)} reshape(f32[10,16,16,16]{3,2,1,0:T(8,128)} %copy.21) | data formatting | bytes 327680 | tf_op jit(solution)/shard_map/reshape | solution.py:484
  46.8 0.0 copy-done.6
  46.8 0.3 fusion.3
  47.2 0.0 copy-done.8
  47.2 0.1 broadcast_in_dim.19
  47.3 0.1 broadcast_in_dim.20
  47.3 0.0 copy-done.7
  47.4 0.3 fusion
  47.7 0.8 %copy.22 = f32[2,5,4096]{2,0,1:T(2,128)} copy(f32[2,5,4096]{2,1,0:T(8,128)S(1)} %reshape.16) | data formatting | bytes 327680 | tf_op jit(solution)/shard_map/reshape | solution.py:492
  (5 shorter events, 0.1 us)
Async XLA Ops:
  2.4 1.1 %copy-start = (bf16[256,1536]{1,0:T(8,128)(2,1)S(1)}, bf16[256,1536]{1,0:T(8,128)(2,1)}, u32[]{:S(2)}) copy-start(bf16[256,1536]{1,0:T(8,128)(2,1)} %constant.48.clone.tan_ref) | copy-start | bytes 2359300
  2.4 1.1 %copy-start.1 = (bf16[2,96,80]{2,1,0:T(8,128)(2,1)S(1)}, bf16[2,96,80]{2,1,0:T(8,128)(2,1)}, u32[]{:S(2)}) copy-start(bf16[2,96,80]{2,1,0:T(8,128)(2,1)} %constant.49.clone.pick_ref) | copy-start | bytes 92164
  2.5 1.1 %copy-start.2 = (s32[5,49]{1,0:T(8,128)S(1)}, s32[5,49]{1,0:T(8,128)}, u32[]{:S(2)}) copy-start(s32[5,49]{1,0:T(8,128)} %send_ref.1) | copy-start | bytes 2944
  2.5 1.1 %copy-start.3 = (s32[2]{0:T(128)S(1)}, s32[2]{0:T(128)}, u32[]{:S(2)}) copy-start(s32[2]{0:T(128)} %level_ref.3) | copy-start | bytes 28
  2.8 3.3 %copy-start.4 = (s32[48]{0:T(128)S(1)}, s32[48]{0:T(128)}, u32[]{:S(2)}) copy-start(s32[48]{0:T(128)} %recv_ref.1) | copy-start | bytes 580
  2.8 3.3 %copy-start.5 = (s32[2]{0:T(128)S(1)}, s32[2]{0:T(128)}, u32[]{:S(2)}) copy-start(s32[2]{0:T(128)} %mig_ref.1) | copy-start | bytes 28
  45.0 1.8 %copy-start.6 = (f32[256,256,1]{1,0,2:T(8,128)S(1)}, f32[256,256,1]{1,0,2:T(8,128)}, u32[]{:S(2)}) copy-start(f32[256,256,1]{1,0,2:T(8,128)} %constant.58) | copy-start | bytes 786436
  45.0 2.2 %copy-start.8 = (s32[2]{0:T(128)S(1)}, s32[2]{0:T(128)}, u32[]{:S(2)}) copy-start(s32[2]{0:T(128)} %param.15) | copy-start | bytes 28
  45.0 2.3 %copy-start.7 = (f32[16,16,1]{1,0,2:T(8,128)S(1)}, f32[16,16,1]{1,0,2:T(8,128)}, u32[]{:S(2)}) copy-start(f32[16,16,1]{1,0,2:T(8,128)} %constant.59) | copy-start | bytes 3076
where the time goes:
time: 48.8 us; the launch traced here: 48.5 us
  Pallas kernels  35.7 us (73%)
  local copies, waits for them, and re-layouts  12 us (25%)
  matrix products  0.59 us (1%)
    pallas_call x1, Pallas kernels, body(): pl.pallas_call(functools.partial(exchange_kernel, nz, n_node, n_core), ou...  29.7 us
    pallas_call x1, Pallas kernels, body(): pl.pallas_call(update_kernel, out_shape=jax.ShapeDtypeStruct((3, 10, 16,...  3.36 us
    pallas_call x1, Pallas kernels, body(): pl.pallas_call(slab_kernel, out_shape=(jax.ShapeDtypeStruct((SLOTS, 8, 12...  2.61 us
    reshape x1, local copies, waits for them, and re-layouts, body(): jnp.transpose(parts[2].reshape(10, 16, 16, 16), (0, 2, 3, 1))  1.83 us
    reshape x1, local copies, waits for them, and re-layouts, body(): jnp.transpose(parts[1].reshape(10, 16, 16, 16), (0, 2, 1, 3))  1.78 us
    unnamed x19, local copies, waits for them, and re-layouts  1.64 us
    transpose x1, local copies, waits for them, and re-layouts, body(): jnp.transpose(parts[2].reshape(10, 16, 16, 16), (0, 2, 3, 1))  1.62 us
    transpose x1, local copies, waits for them, and re-layouts, body(): jnp.transpose(parts[1].reshape(10, 16, 16, 16), (0, 2, 1, 3))  1.49 us

commit v1 on v0

v1 whole, which is shorter than its diff:
```python
import functools

import jax
import jax.numpy as jnp
import numpy as np
from jax import lax
from jax.experimental import pallas as pl
from jax.experimental.pallas import tpu as pltpu
from jax.sharding import PartitionSpec as P

MESH = pl.DeviceIdType.MESH
F32 = jnp.float32
BF16 = jnp.bfloat16
EDGE = 16
REACH = 3
CAP = 7
SLOTS = 49
VM = pl.BlockSpec(memory_space=pltpu.VMEM)
SM = pl.BlockSpec(memory_space=pltpu.SMEM)
HB = pl.BlockSpec(memory_space=pltpu.HBM)


def predict_table(n):
    w = np.zeros((2 * n, n))
    for c in range(n):
        w[2 * c, c] = 1.0
        if c == 0:
            w[1, 0:4] = np.array([5.0, 15.0, -5.0, 1.0]) / 16.0
        elif c == n - 2:
            w[2 * c + 1, n - 4 : n] = np.array([1.0, -5.0, 15.0, 5.0]) / 16.0
        elif c == n - 1:
            w[2 * c + 1, n - 1] = 1.0
        else:
            w[2 * c + 1, c - 1 : c + 3] = np.array([-1.0, 9.0, 9.0, -1.0]) / 16.0
    return w


def window_tables():
    depth = np.zeros((3, 3, 5))
    depth[0, :, 0:3] = np.eye(3)
    depth[1, :, 0:4] = predict_table(8)[0:3, 0:4]
    depth[2, 0, 0] = depth[2, 1, 2] = depth[2, 2, 4] = 1.0
    eye, fine = np.eye(16), predict_table(16)
    tangent = np.zeros((3, 4, 8, 16))
    for s in range(4):
        tangent[0, s] = eye[8 * (s % 2) : 8 * (s % 2) + 8]
        tangent[1, s] = fine[8 * s : 8 * s + 8]
        tangent[2, s] = eye[0::2]
    return depth, tangent


def constant_tables():
    depth, tangent = window_tables()
    pairs = [(0, s, 0) for s in range(2)]
    pairs += [(1, s, 2 * t) for s in range(4) for t in range(2)]
    pairs += [(2, 0, 0)]
    cols = []
    for kind, sa, sb in pairs:
        tile = np.zeros((16, 16, 8, 2, 8))
        for parity in range(2):
            tile[:, :, :, parity, :] = np.einsum(
                "pa,qb->abpq", tangent[kind, sa], tangent[kind, sb + parity]
            )
        cols.append(tile.reshape(256, 128))
    cols.append(np.zeros((256, 128)))
    tangents = np.concatenate(cols, 1)
    picks = np.zeros((2, 3, 2, 16, 10, 8))
    for kind in range(3):
        for b in range(2):
            for f in range(5):
                for i in range(3):
                    for layer in range(5):
                        picks[0, kind, b, f * 3 + i, b * 5 + f, layer] = depth[kind, i, layer]
                        picks[1, kind, b, f * 3 + i, b * 5 + f, 7 - layer] = depth[kind, i, layer]
    return tangents, picks.reshape(2, 96, 80)


def three_parts(x):
    high = x.astype(BF16)
    rest = x - high.astype(F32)
    middle = rest.astype(BF16)
    low = (rest - middle.astype(F32)).astype(BF16)
    return high, middle, low


def dot(a, b):
    return jnp.dot(a, b, preferred_element_type=F32)


def iotas():
    lane = lax.broadcasted_iota(jnp.int32, (8, 128), 1)
    row = lax.broadcasted_iota(jnp.int32, (8, 128), 0)
    return lane, row


def swap(planes, lane, bit, reach):
    keep = (lane & reach) == 0
    out = list(planes)
    for v in range(8):
        if not (v >> bit) & 1:
            w = v | (1 << bit)
            out[v] = jnp.where(keep, planes[v], pltpu.roll(planes[w], reach, 1))
            out[w] = jnp.where(keep, pltpu.roll(planes[v], 128 - reach, 1), planes[w])
    return out


def swaps(planes, lane, reach):
    for bit in (2, 1, 0):
        planes = swap(planes, lane, bit, reach << bit)
    return planes


def cross(x, lane, row):
    odd = row & 1
    low = jnp.where(odd == 0, x, pltpu.roll(x, 1, 0))
    high = jnp.where(odd == 0, pltpu.roll(x, 7, 0), x)
    index = (lane & 7) * 16 + odd * 8 + lax.shift_right_logical(lane, 4)
    return jnp.where(
        (lane & 8) == 0,
        jnp.take_along_axis(low, index, axis=1),
        jnp.take_along_axis(high, index, axis=1),
    )


def turned(planes, dim, lane, row):
    if dim == 1:
        return swaps(planes, lane, 16)
    return [cross(x, lane, row) for x in swaps(planes, lane, 1)]


def turned_back(planes, dim, lane, row):
    if dim == 1:
        return swaps(planes, lane, 16)
    return swaps([cross(x, lane, row) for x in planes], lane, 1)


def row_of(dim, half, block, h):
    return half * 4 + block * 2 + h if dim == 0 else h * 4 + block * 2 + half


def plane_rows(ref, dim, half, base=0):
    return jnp.concatenate(
        [
            jnp.concatenate(
                [ref[pl.ds(base + f * 64 + row_of(dim, half, b, h), 8, stride=8), :] for h in range(2)], 1
            )
            for b in range(2)
            for f in range(5)
        ],
        0,
    )


def exchange_kernel(
    nz, n_node, n_core,
    x_ref, send_ref, recv_ref, mig_ref, level_ref, tan_hbm, pick_hbm,
    dense_ref, ghost_ref, moved_ref, top_ref,
    turns, left, wide, slabs, got, want_out, want_in, stage_g, stage_x, peak, peaks,
    tan_ref, pick_ref, slab_s, slab_r, want_s, want_r, move_s, move_r, peak_s, peak_r, load_s,
):
    node, core = lax.axis_index("node"), lax.axis_index("cores")
    me = node * n_core + core
    total = n_node * n_core
    ny = n_node // nz
    z, y = node % nz, node // nz
    lane, row = iotas()

    def along(offset):
        other = (me + offset + total) % total
        return (other // n_core, other % n_core)

    groups = [
        [(node, (core + t) % n_core) for t in range(1, n_core)],
        [(y * nz + (z + t) % nz, core) for t in range(1, nz)],
        [(((y + t) % ny) * nz + z, core) for t in range(1, ny)],
    ]
    offsets = [o for o in range(-REACH, REACH + 1) if o != 0]
    partners = [d for group in groups for d in group] + [along(o) for o in offsets]
    barrier = pltpu.get_barrier_semaphore()
    for d in partners:
        pl.semaphore_signal(barrier, inc=1, device_id=d, device_id_type=MESH)
    load_pick = pltpu.make_async_copy(pick_hbm, pick_ref, load_s.at[0])
    load_tan = pltpu.make_async_copy(tan_hbm, tan_ref, load_s.at[1])
    load_pick.start()
    load_tan.start()

    def send_peaks(phase):
        base = sum(len(g) for g in groups[:phase])
        copies = [
            pltpu.make_async_remote_copy(
                src_ref=peak.at[phase],
                dst_ref=peaks.at[base + t],
                send_sem=peak_s.at[base + t],
                recv_sem=peak_r.at[base + t],
                device_id=d,
                device_id_type=MESH,
            )
            for t, d in enumerate(groups[phase])
        ]
        for c in copies:
            c.start()
        return copies

    def take_peaks(phase, copies):
        base = sum(len(g) for g in groups[:phase])
        for c in copies:
            c.wait_recv()
        best = peak[phase]
        for t in range(len(copies)):
            best = jnp.maximum(best, peaks[base + t])
        return best

    for f in range(5):
        for c in range(32):
            at = f * 64 + (c // 2 % 8) * 8 + (c // 16) * 4 + c % 2
            turns[pl.ds(at, 2, stride=2), :] = x_ref[f, :, c * 128 : c * 128 + 128]
    top = None
    for v in range(8):
        u = [turns[f * 64 + v * 8 : f * 64 + v * 8 + 8] for f in range(5)]
        inv = 1.0 / u[0]
        vel = [u[1 + i] * inv for i in range(3)]
        kinetic = u[1] * vel[0] + u[2] * vel[1] + u[3] * vel[2]
        pressure = 0.4 * (u[4] - 0.5 * kinetic)
        speed = jnp.maximum(jnp.maximum(jnp.abs(vel[0]), jnp.abs(vel[1])), jnp.abs(vel[2]))
        speed = speed + jnp.sqrt(1.4 * pressure * inv)
        top = speed if v == 0 else jnp.maximum(top, speed)
    scales = [lax.shift_left(jnp.int32(EDGE), level_ref[b]).astype(F32) for b in range(2)]
    rated = top * jnp.where((row & 2) == 0, scales[0], scales[1])
    peak[0, 0:8] = jnp.full((8, 128), jnp.max(top), F32)
    peak[0, 8:16] = jnp.full((8, 128), jnp.max(rated), F32)
    for n, direction in enumerate((1, -1)):
        want = jnp.int32(0)
        for j in range(2):
            source = mig_ref[j]
            want = want + jnp.where(source // 2 == me + direction, source % 2, 0)
        want_out[n] = jnp.full((8, 128), want, jnp.int32).astype(F32)
    pl.semaphore_wait(barrier, len(partners))
    first = send_peaks(0)
    want_copies = [
        pltpu.make_async_remote_copy(
            src_ref=want_out.at[n],
            dst_ref=want_in.at[n],
            send_sem=want_s.at[n],
            recv_sem=want_r.at[n],
            device_id=along(direction),
            device_id_type=MESH,
        )
        for n, direction in enumerate((1, -1))
    ]
    for c in want_copies:
        c.start()
    for f in range(5):
        planes = [turns[f * 64 + v * 8 : f * 64 + v * 8 + 8] for v in range(8)]
        for v in range(8):
            dense_ref[f * 64 + v * 8 : f * 64 + v * 8 + 8] = planes[v]
        for dim in (1, 2):
            for v, value in enumerate(turned(planes, dim, lane, row)):
                at = dim * 320 + f * 64 + v * 8
                turns[at : at + 8] = value
    load_pick.wait()
    for g in range(6):
        side = g % 2
        parts = three_parts(plane_rows(turns, g // 2, side, (g // 2) * 320))
        rows = sum(dot(pick_ref[side], part) for part in parts)
        for n, part in enumerate(three_parts(rows)):
            for kind in range(3):
                left[kind, n, g * 32 : g * 32 + 32] = part[kind * 32 : kind * 32 + 32]
    peak[1] = take_peaks(0, first)
    second = send_peaks(1)
    load_tan.wait()
    for tile in range(6):
        kind = 0 if tile == 0 else 1 if tile < 5 else 2
        weights = tan_ref[:, tile * 256 : tile * 256 + 256]
        out = sum(dot(left[kind, n], weights) for n in range(3))
        wide[2 * tile] = out[:, 0:128].reshape(12, 16, 128)
        if tile < 5:
            wide[2 * tile + 1] = out[:, 128:256].reshape(12, 16, 128)
    even = (lane & 8) == 0

    def entry(k, into, at):
        blk, g, kind = send_ref[0, k], send_ref[1, k], send_ref[2, k]
        sa, sb = send_ref[3, k], send_ref[4, k]
        pair = jnp.where(kind == 0, sa % 2, jnp.where(kind == 1, 2 + sa * 2 + sb // 2, 10))
        parity = jnp.where(kind == 2, 0, sb % 2)
        low = wide[pair, g * 2 + blk, 0:8]
        high = wide[pair, g * 2 + blk, 8:16]
        ahead = jnp.where(even, low, pltpu.roll(high, 8, 1))
        behind = jnp.where(even, pltpu.roll(low, 120, 1), high)
        into[at] = jnp.where(jnp.full((8, 128), parity, jnp.int32) == 0, ahead, behind)

    slab_copies = []
    for n, o in enumerate(offsets):
        for m in range(CAP):
            entry((o + REACH) * CAP + m, slabs, n * CAP + m)
        copy = pltpu.make_async_remote_copy(
            src_ref=slabs.at[pl.ds(n * CAP, CAP)],
            dst_ref=got.at[pl.ds((REACH - o) * CAP, CAP)],
            send_sem=slab_s.at[n],
            recv_sem=slab_r.at[n],
            device_id=along(o),
            device_id_type=MESH,
        )
        copy.start()
        slab_copies.append(copy)
    for m in range(CAP):
        entry(REACH * CAP + m, got, REACH * CAP + m)
    peak[2] = take_peaks(1, second)
    third = send_peaks(2)
    for c in want_copies + slab_copies:
        c.wait_recv()
    second_block = [want_in[n] > 0.5 for n in range(2)]
    for n in range(2):
        pick = second_block[n]
        for f in range(5):
            for t in range(4):
                at = f * 64 + t * 16
                one, two = turns[at : at + 8], turns[at + 8 : at + 16]
                one = jnp.where(pick, pltpu.roll(one, 6, 0), one)
                two = jnp.where(pick, two, pltpu.roll(two, 2, 0))
                stage_x[n, f, t] = jnp.where((row & 2) == 0, one, two)
    move_copies = []
    for n, direction in enumerate((-1, 1)):
        for m, (src, dst) in enumerate(
            (
                (stage_x.at[n], moved_ref.at[1 - n]),
                (stage_g.at[n], ghost_ref.at[3 - n]),
            )
        ):
            move_copies.append(
                pltpu.make_async_remote_copy(
                    src_ref=src,
                    dst_ref=dst,
                    send_sem=move_s.at[2 * n + m],
                    recv_sem=move_r.at[2 * n + m],
                    device_id=along(direction),
                    device_id_type=MESH,
                )
            )
    move_copies[0].start()
    move_copies[2].start()
    for g in range(6):
        for qa in range(2):
            pair = []
            for b in range(2):
                at = (b * 6 + g) * 4 + 2 * qa
                one, two = got[recv_ref[at]], got[recv_ref[at + 1]]
                low = jnp.where(even, one, pltpu.roll(two, 8, 1))
                high = jnp.where(even, pltpu.roll(one, 120, 1), two)
                high = jnp.where(row == 7, scales[b], high)
                ghost_ref[b, g, qa, 0:8] = low
                ghost_ref[b, g, qa, 8:16] = high
                pair.append((low, high))
            for n in range(2):
                pick = second_block[n]
                stage_g[n, g, qa, 0:8] = jnp.where(pick, pair[1][0], pair[0][0])
                stage_g[n, g, qa, 8:16] = jnp.where(pick, pair[1][1], pair[0][1])
    move_copies[1].start()
    move_copies[3].start()
    top_ref[...] = take_peaks(2, third)
    for c in move_copies:
        c.wait_recv()
    for c in first + second + third + want_copies + slab_copies + move_copies:
        c.wait_send()


def weno(values, centres, mirrored):
    half = 0.5 * (values[1:] - values[:-1])
    bend = half[1:] - half[:-1]
    rough = 1e-6 + (13.0 / 3.0) * (bend * bend)
    third = bend * (1.0 / 3.0)
    lo, n = centres, 9
    gl, gr = half[lo - 1 : lo - 1 + n], half[lo : lo + n]
    bl, bc, br = (slice(lo - 2 + t, lo - 2 + t + n) for t in range(3))
    tl = 2.0 * gl + bend[bl]
    tc = gl + gr
    tr = 2.0 * gr - bend[br]
    sl = rough[bl] + tl * tl
    sc = rough[bc] + tc * tc
    sr = rough[br] + tr * tr
    il = pl.reciprocal(sl, approx=True)
    ic = pl.reciprocal(sc, approx=True)
    ir = pl.reciprocal(sr, approx=True)
    wl, wc, wr = il * il, 6.0 * (ic * ic), ir * ir
    if mirrored:
        wl = 3.0 * wl
        cl = third[bl] + gl
        cc = third[bc] + gl
        cr = gr - 2.0 * third[br]
        total = wl * cl + wc * cc + wr * cr
        sign = -1.0
    else:
        wr = 3.0 * wr
        cl = gl + 2.0 * third[bl]
        cc = gr - third[bc]
        cr = gr - third[br]
        total = wl * cl + wc * cc + wr * cr
        sign = 1.0
    share = total * pl.reciprocal(wl + wc + wr, approx=True)
    centre = values[lo : lo + n]
    return centre + share if sign > 0 else centre - share


def update_kernel(
    n_core, dense_ref, moved_ref, ghost_ref, top_ref, mig_ref, flag_ref, lane_hbm, line_hbm, out_ref,
    cells, rims, plus, minus, change, result, lane_ref, line_ref, load_s,
):
    load_lane = pltpu.make_async_copy(lane_hbm, lane_ref, load_s.at[0])
    load_line = pltpu.make_async_copy(line_hbm, line_ref, load_s.at[1])
    load_lane.start()
    load_line.start()
    me = lax.axis_index("node") * n_core + lax.axis_index("cores")
    lane, row = iotas()
    slots = []
    for j in range(2):
        source = mig_ref[j]
        far = jnp.where(source // 2 < me, 2, 3)
        slots.append(jnp.where(source // 2 == me, source % 2, far))
    for b in range(2):
        for g in range(6):
            for h in range(2):
                base = (g // 2) * 128 + row_of(g // 2, g % 2, b, h)
                rims[pl.ds(base, 8, stride=8), :] = ghost_ref[slots[b], g, h, 0:8]
                rims[pl.ds(base + 64, 8, stride=8), :] = ghost_ref[slots[b], g, h, 8:16]
    for f in range(5):
        planes = []
        for v in range(8):
            own = dense_ref[f * 64 + v * 8 : f * 64 + v * 8 + 8]
            down, up = moved_ref[0, f, v // 2], moved_ref[1, f, v // 2]
            for b in range(2):
                away = 6 if b == 0 else 2
                mine = jnp.where(slots[b] == b, own, pltpu.roll(own, away, 0))
                other = jnp.where(slots[b] == 2, down, up)
                if v % 2 != b:
                    other = pltpu.roll(other, away, 0)
                value = jnp.where(slots[b] < 2, mine, other)
                both = value if b == 0 else jnp.where((row & 2) == 0, both, value)
            planes.append(both)
        for a in range(3):
            layout = planes if a == 0 else turned(planes, a, lane, row)
            lower = (row & (4 if a == 0 else 1)) == 0
            up, down = (4, 4) if a == 0 else (1, 7)
            for v in range(8):
                cells[a, f, 3 + v] = layout[v]
            for layer in range(3):
                rim = rims[a * 128 + (f * 3 + layer) * 8 : a * 128 + (f * 3 + layer) * 8 + 8]
                cells[a, f, 2 - layer] = jnp.where(lower, rim, pltpu.roll(layout[7 - layer], up, 0))
                cells[a, f, 11 + layer] = jnp.where(lower, pltpu.roll(layout[layer], down, 0), rim)
    fastest = top_ref[0:8]
    step = 0.4 / top_ref[8:16]
    factor = step * rims[120:128]
    for a in range(3):

        def flux(p, carry):
            u = [cells[a, f, p] for f in range(5)]
            inv = 1.0 / u[0]
            v = [u[1 + i] * inv for i in range(3)]
            kinetic = u[1] * v[0] + u[2] * v[1] + u[3] * v[2]
            pressure = 0.4 * (u[4] - 0.5 * kinetic)
            flow = [u[1 + a]] + [u[1 + i] * v[a] for i in range(3)] + [(u[4] + pressure) * v[a]]
            flow[1 + a] = flow[1 + a] + pressure
            for f in range(5):
                plus[f, p] = 0.5 * (flow[f] + fastest * u[f])
                minus[f, p] = 0.5 * (flow[f] - fastest * u[f])
            return carry

        lax.fori_loop(0, 14, flux, 0, unroll=2)

        def field(f, carry):
            hat = weno(plus[f], 2, False) + weno(minus[f], 3, True)
            change[a, f] = hat[1:] - hat[:-1]
            return carry

        lax.fori_loop(0, 5, field, 0)
    for f in range(5):
        second = turned_back([change[1, f, v] for v in range(8)], 1, lane, row)
        third = turned_back([change[2, f, v] for v in range(8)], 2, lane, row)
        for v in range(8):
            moved = change[0, f, v] + second[v] + third[v]
            result[f * 64 + v * 8 : f * 64 + v * 8 + 8] = cells[0, f, 3 + v] - factor * moved

    load_lane.wait()
    load_line.wait()

    @pl.when(jnp.logical_or(flag_ref[0] == 1, flag_ref[1] == 1))
    def _():
        halves = [plane_rows(result, 0, half) for half in range(2)]
        cubes = jnp.concatenate(
            [halves[half][n * 8 : n * 8 + 8] for n in range(10) for half in range(2)], 0
        )
        smooth = sum(dot(part, lane_ref[...]) for part in three_parts(cubes))
        smooth = sum(dot(line_ref[...], part) for part in three_parts(smooth))
        for b in range(2):

            @pl.when(flag_ref[b] == 1)
            def _():
                for f in range(5):
                    for half in range(2):
                        at = (b * 5 + f) * 16 + half * 8
                        for h in range(2):
                            base = f * 64 + row_of(0, half, b, h)
                            result[pl.ds(base, 8, stride=8), :] = smooth[at : at + 8, h * 128 : h * 128 + 128]

    for f in range(5):
        for c in range(32):
            at = f * 64 + (c // 2 % 8) * 8 + (c // 16) * 4 + c % 2
            out_ref[f, :, c * 128 : c * 128 + 128] = result[pl.ds(at, 2, stride=2), :]


def solution(mesh):
    n_node, n_core = mesh.shape["node"], mesh.shape["cores"]
    nz = max(1, int(round(n_node**0.5)))
    tangents, picks = constant_tables()
    smoother = predict_table(8) @ np.eye(16)[0::2]
    lane_smoother = np.kron(smoother, smoother).T
    line_smoother = np.kron(np.eye(10), smoother)
    groups = n_core - 1 + nz - 1 + n_node // nz - 1

    def body(block_state, levels, send_table, receive_table, migration, coarsen_flags):
        dense, ghosts, moved, top = pl.pallas_call(
            functools.partial(exchange_kernel, nz, n_node, n_core),
            out_shape=(
                jax.ShapeDtypeStruct((320, 128), F32),
                jax.ShapeDtypeStruct((4, 6, 2, 16, 128), F32),
                jax.ShapeDtypeStruct((2, 5, 4, 8, 128), F32),
                jax.ShapeDtypeStruct((16, 128), F32),
            ),
            in_specs=[VM, SM, SM, SM, SM, HB, HB],
            out_specs=(VM, VM, VM, VM),
            scratch_shapes=[
                pltpu.VMEM((960, 128), F32),
                pltpu.VMEM((3, 3, 192, 256), BF16),
                pltpu.VMEM((11, 12, 16, 128), F32),
                pltpu.VMEM((SLOTS - CAP, 8, 128), F32),
                pltpu.VMEM((SLOTS, 8, 128), F32),
                pltpu.VMEM((2, 8, 128), F32),
                pltpu.VMEM((2, 8, 128), F32),
                pltpu.VMEM((2, 6, 2, 16, 128), F32),
                pltpu.VMEM((2, 5, 4, 8, 128), F32),
                pltpu.VMEM((3, 16, 128), F32),
                pltpu.VMEM((groups, 16, 128), F32),
                pltpu.VMEM((256, 1536), BF16),
                pltpu.VMEM((2, 96, 80), BF16),
                pltpu.SemaphoreType.DMA((6,)),
                pltpu.SemaphoreType.DMA((6,)),
                pltpu.SemaphoreType.DMA((2,)),
                pltpu.SemaphoreType.DMA((2,)),
                pltpu.SemaphoreType.DMA((4,)),
                pltpu.SemaphoreType.DMA((4,)),
                pltpu.SemaphoreType.DMA((groups,)),
                pltpu.SemaphoreType.DMA((groups,)),
                pltpu.SemaphoreType.DMA((2,)),
            ],
            compiler_params=pltpu.CompilerParams(
                collective_id=0, has_side_effects=True, vmem_limit_bytes=48 << 20
            ),
            name="exchange",
        )(
            jnp.transpose(block_state, (1, 0, 2)), send_table, receive_table, migration, levels,
            jnp.asarray(tangents, BF16), jnp.asarray(picks, BF16),
        )
        state = pl.pallas_call(
            functools.partial(update_kernel, n_core),
            out_shape=jax.ShapeDtypeStruct((5, 2, 4096), F32),
            in_specs=[VM, VM, VM, VM, SM, SM, HB, HB],
            out_specs=VM,
            scratch_shapes=[
                pltpu.VMEM((3, 5, 14, 8, 128), F32),
                pltpu.VMEM((3 * 16 * 8, 128), F32),
                pltpu.VMEM((5, 14, 8, 128), F32),
                pltpu.VMEM((5, 14, 8, 128), F32),
                pltpu.VMEM((3, 5, 8, 8, 128), F32),
                pltpu.VMEM((320, 128), F32),
                pltpu.VMEM((256, 256), BF16),
                pltpu.VMEM((160, 160), BF16),
                pltpu.SemaphoreType.DMA((2,)),
            ],
            compiler_params=pltpu.CompilerParams(vmem_limit_bytes=48 << 20),
            name="update",
        )(
            dense, moved, ghosts, top, migration, coarsen_flags,
            jnp.asarray(lane_smoother, BF16), jnp.asarray(line_smoother, BF16),
        )
        return jnp.transpose(state, (1, 0, 2))

    both = ("node", "cores")
    return jax.shard_map(
        body,
        mesh=mesh,
        in_specs=(P(both, None, None), P(both), P(None, both), P(both), P(both), P(both)),
        out_specs=P(both, None, None),
        check_vma=False,
    )
```

time: 48.8 us -> 43 us (0.88)
  local copies, waits for them, and re-layouts: 12 us -> 4.85 us
  Pallas kernels: 35.7 us -> 37.8 us
  matrix products: 0.59 us -> 0 us
    reshape x5 -> x0, local copies, waits for them, and re-layouts: 4.88 us -> none  [the longest x1 1.83 us: body(): jnp.transpose(parts[2].reshape(10, 16, 16, 16), (0, 2, 3, 1))]
    transpose x3 -> x0, local copies, waits for them, and re-layouts: 3.52 us -> none  [the longest x1 1.62 us: body(): jnp.transpose(parts[2].reshape(10, 16, 16, 16), (0, 2, 3, 1))]
    unnamed x19 -> x20, local copies, waits for them, and re-layouts: 1.64 us -> 4.85 us
    another operation x5 -> x0, local copies, waits for them, and re-layouts: 1.79 us -> none  [the longest x3 1.01 us: body(): jnp.stack([cube.reshape(10, 16, 256), jnp.transpose(cube, (0, 2, 1, 3)).r...]
    pallas_call x1, Pallas kernels: 29.7 us -> 31.4 us  [body(): pl.pallas_call(functools.partial(exchange_kernel, nz, n_node, n_core), ou...]
    dot_general x2 -> x0, matrix products: 0.59 us -> none  [the longest x1 0.31 us: body(): jnp.einsum('nim,mt->nit', migrated, jnp.asarray(plane_smoother.T, F32), p...]
    pallas_call x2 -> x1, Pallas kernels: 5.97 us -> 6.42 us  [body(): pl.pallas_call(functools.partial(update_kernel, n_core), out_shape=jax.Sh...]
where the time goes in v1:
time: 43 us; the launch traced here: 42.7 us
  Pallas kernels  37.8 us (88%)
  local copies, waits for them, and re-layouts  4.85 us (11%)
    pallas_call x1, Pallas kernels, body(): pl.pallas_call(functools.partial(exchange_kernel, nz, n_node, n_core), ou...  31.4 us
    pallas_call x1, Pallas kernels, body(): pl.pallas_call(functools.partial(update_kernel, n_core), out_shape=jax.Sh...  6.42 us
    unnamed x20, local copies, waits for them, and re-layouts  4.85 us

profile of v1, /device:TPU:1, one launch (start us, length us, event | category | flops | bytes accessed | tf_op | source)
XLA Modules:
  0.0 42.7 jit_solution(5209862836299483991)
XLA Ops:
  0.0 0.0 copy-start.6
  0.0 0.0 copy-start.8
  0.0 0.0 copy-start.9
  0.0 0.6 %copy-done.6 = s32[2]{0:T(128)S(1)} copy-done((s32[2]{0:T(128)S(1)}, s32[2]{0:T(128)}, u32[]{:S(2)}) %copy-start.6) | copy-done | bytes 32
  0.7 0.0 copy-done.8
  0.7 0.0 copy-done.9
  0.7 0.0 copy-start
  0.7 1.1 %copy-done = bf16[256,1536]{1,0:T(8,128)(2,1)S(1)} copy-done((bf16[256,1536]{1,0:T(8,128)(2,1)S(1)}, bf16[256,1536]{1,0:T(8,128)(2,1)}, u32[]{:S(2)}) %copy-start) | copy-done | bytes 786456
  1.8 0.0 copy-start.1
  1.8 0.9 %copy-done.1 = f32[2,5,4096]{2,0,1:T(2,128)S(1)} copy-done((f32[2,5,4096]{2,0,1:T(2,128)S(1)}, f32[2,5,4096]{2,0,1:T(2,128)}, u32[]{:S(2)}) %copy-start.1) | copy-done | bytes 163864
  2.7 0.0 copy-start.4
  2.7 0.8 %copy-done.4 = bf16[2,96,80]{2,1,0:T(8,128)(2,1)S(1)} copy-done((bf16[2,96,80]{2,1,0:T(8,128)(2,1)S(1)}, bf16[2,96,80]{2,1,0:T(8,128)(2,1)}, u32[]{:S(2)}) %copy-start.4) | copy-done | bytes 30744
  3.5 0.0 copy-start.5
  3.5 0.7 %copy-done.5 = s32[5,49]{1,0:T(8,128)S(1)} copy-done((s32[5,49]{1,0:T(8,128)S(1)}, s32[5,49]{1,0:T(8,128)}, u32[]{:S(2)}) %copy-start.5) | copy-done | bytes 1004
  4.2 0.0 copy-start.2
  4.2 0.0 copy-start.3
  4.2 31.4 %exchange.1 = (f32[320,128]{1,0:T(8,128)S(1)}, f32[4,6,2,16,128]{4,3,2,1,0:T(8,128)S(1)}, f32[2,5,4,8,128]{4,3,2,1,0:T(8,128)S(1)}, f32[16,128]{1,0:T(8,128)S(1)}) custom-call(f32[5,2,4096]{2,1,0:T(2,128)S(1)} %bitcast.2, s32[5,49]{1,0:T(8,128)S(1)} %copy-done.5, s32[48]{0:T(128)S(1)} %copy-done.8, s32[2]{0:T(128)S(1)} %copy-done.6, s32[2]{0:T(128)S(1)} %copy-done.9, ...), custom_call_target="tpu_custom_call" | custom-call | tf_op jit(solution)/shard_map/exchange/pallas_call | solution.py:519
  35.6 0.0 copy-start.7
  35.6 0.0 copy-done.2
  35.6 0.0 copy-done.3
  35.7 0.6 %copy-done.7 = s32[2]{0:T(128)S(1)} copy-done((s32[2]{0:T(128)S(1)}, s32[2]{0:T(128)}, u32[]{:S(2)}) %copy-start.7) | copy-done | bytes 32
  36.3 6.4 %update.1 = f32[5,2,4096]{2,1,0:T(2,128)} custom-call(f32[320,128]{1,0:T(8,128)S(1)} %get-tuple-element.9.dense_ref, f32[2,5,4,8,128]{4,3,2,1,0:T(8,128)S(1)} %get-tuple-element.10.moved_ref, f32[4,6,2,16,128]{4,3,2,1,0:T(8,128)S(1)} %get-tuple-element.11.ghost_ref, f32[16,128]{1,0:T(8,128)S(1)} %get-tuple-element.12.top_ref, s32[2]{0:T(128)S(1)} %copy-done.6, ...), custom_call_target="tpu_custom_call" | custom-call | tf_op jit(solution)/shard_map/update/pallas_call | solution.py:561
Async XLA Ops:
  0.0 0.7 %copy-start.6 = (s32[2]{0:T(128)S(1)}, s32[2]{0:T(128)}, u32[]{:S(2)}) copy-start(s32[2]{0:T(128)} %mig_ref.3) | copy-start | bytes 28
  0.0 0.7 %copy-start.8 = (s32[48]{0:T(128)S(1)}, s32[48]{0:T(128)}, u32[]{:S(2)}) copy-start(s32[48]{0:T(128)} %recv_ref.1) | copy-start | bytes 580
  0.0 0.7 %copy-start.9 = (s32[2]{0:T(128)S(1)}, s32[2]{0:T(128)}, u32[]{:S(2)}) copy-start(s32[2]{0:T(128)} %level_ref.1) | copy-start | bytes 28
  0.7 1.1 %copy-start = (bf16[256,1536]{1,0:T(8,128)(2,1)S(1)}, bf16[256,1536]{1,0:T(8,128)(2,1)}, u32[]{:S(2)}) copy-start(bf16[256,1536]{1,0:T(8,128)(2,1)} %constant.8.clone.tan_hbm) | copy-start | bytes 2359300
  1.8 0.9 %copy-start.1 = (f32[2,5,4096]{2,0,1:T(2,128)S(1)}, f32[2,5,4096]{2,0,1:T(2,128)}, u32[]{:S(2)}) copy-start(f32[2,5,4096]{2,0,1:T(2,128)} %param.10) | copy-start | bytes 491524
  2.7 0.8 %copy-start.4 = (bf16[2,96,80]{2,1,0:T(8,128)(2,1)S(1)}, bf16[2,96,80]{2,1,0:T(8,128)(2,1)}, u32[]{:S(2)}) copy-start(bf16[2,96,80]{2,1,0:T(8,128)(2,1)} %constant.9.clone.pick_hbm) | copy-start | bytes 92164
  3.5 0.7 %copy-start.5 = (s32[5,49]{1,0:T(8,128)S(1)}, s32[5,49]{1,0:T(8,128)}, u32[]{:S(2)}) copy-start(s32[5,49]{1,0:T(8,128)} %send_ref.1) | copy-start | bytes 2944
  4.2 31.4 %copy-start.2 = (bf16[256,256]{1,0:T(8,128)(2,1)S(1)}, bf16[256,256]{1,0:T(8,128)(2,1)}, u32[]{:S(2)}) copy-start(bf16[256,256]{1,0:T(8,128)(2,1)} %constant.10.clone.lane_hbm) | copy-start | bytes 393220
  4.2 31.4 %copy-start.3 = (bf16[160,160]{1,0:T(8,128)(2,1)S(1)}, bf16[160,160]{1,0:T(8,128)(2,1)}, u32[]{:S(2)}) copy-start(bf16[160,160]{1,0:T(8,128)(2,1)} %constant.11.clone.line_hbm) | copy-start | bytes 153604
  35.6 0.7 %copy-start.7 = (s32[2]{0:T(128)S(1)}, s32[2]{0:T(128)}, u32[]{:S(2)}) copy-start(s32[2]{0:T(128)} %flag_ref.1) | copy-start | bytes 28

commit v2 on v1

--- a/solution.py
+++ b/solution.py
@@ -14,6 +14,7 @@
 EDGE = 16
 REACH = 3
 CAP = 7
+VMEM_BYTES = 63 << 20
 SLOTS = 49
 VM = pl.BlockSpec(memory_space=pltpu.VMEM)
 SM = pl.BlockSpec(memory_space=pltpu.SMEM)
@@ -75,12 +76,14 @@
     return tangents, picks.reshape(2, 96, 80)
 
 
-def three_parts(x):
-    high = x.astype(BF16)
-    rest = x - high.astype(F32)
-    middle = rest.astype(BF16)
-    low = (rest - middle.astype(F32)).astype(BF16)
-    return high, middle, low
+def parts_of(count, x):
+    parts = []
+    for n in range(count):
+        part = x.astype(BF16)
+        parts.append(part)
+        if n < count - 1:
+            x = x - part.astype(F32)
+    return parts
 
 
 def dot(a, b):
@@ -151,12 +154,13 @@
     )
 
 
-def exchange_kernel(
+def section_kernel(
     nz, n_node, n_core,
-    x_ref, send_ref, recv_ref, mig_ref, level_ref, tan_hbm, pick_hbm,
-    dense_ref, ghost_ref, moved_ref, top_ref,
-    turns, left, wide, slabs, got, want_out, want_in, stage_g, stage_x, peak, peaks,
-    tan_ref, pick_ref, slab_s, slab_r, want_s, want_r, move_s, move_r, peak_s, peak_r, load_s,
+    x_hbm, send_ref, recv_ref, mig_ref, level_ref, flag_ref, tan_hbm, pick_hbm, lane_hbm, line_hbm,
+    out_ref,
+    x_ref, turns, left, wide, slabs, got, want_out, want_in, stage_g, stage_x, ghost_ref, moved_ref, peak, peaks,
+    cells, rims, plus, minus, change, result, tan_ref, pick_ref, lane_ref, line_ref,
+    slab_s, slab_r, want_s, want_r, move_s, move_r, peak_s, peak_r, load_s,
 ):
     node, core = lax.axis_index("node"), lax.axis_index("cores")
     me = node * n_core + core
@@ -179,10 +183,13 @@
     barrier = pltpu.get_barrier_semaphore()
     for d in partners:
         pl.semaphore_signal(barrier, inc=1, device_id=d, device_id_type=MESH)
-    load_pick = pltpu.make_async_copy(pick_hbm, pick_ref, load_s.at[0])
-    load_tan = pltpu.make_async_copy(tan_hbm, tan_ref, load_s.at[1])
-    load_pick.start()
-    load_tan.start()
+    load_x = pltpu.make_async_copy(x_hbm, x_ref, load_s.at[0])
+    load_pick = pltpu.make_async_copy(pick_hbm, pick_ref, load_s.at[1])
+    load_tan = pltpu.make_async_copy(tan_hbm, tan_ref, load_s.at[2])
+    load_lane = pltpu.make_async_copy(lane_hbm, lane_ref, load_s.at[3])
+    load_line = pltpu.make_async_copy(line_hbm, line_ref, load_s.at[4])
+    for load in (load_x, load_pick, load_tan, load_lane, load_line):
+        load.start()
 
     def send_peaks(phase):
         base = sum(len(g) for g in groups[:phase])
@@ -210,6 +217,7 @@
             best = jnp.maximum(best, peaks[base + t])
         return best
 
+    load_x.wait()
     for f in range(5):
         for c in range(32):
             at = f * 64 + (c // 2 % 8) * 8 + (c // 16) * 4 + c % 2
@@ -251,8 +259,6 @@
         c.start()
     for f in range(5):
         planes = [turns[f * 64 + v * 8 : f * 64 + v * 8 + 8] for v in range(8)]
-        for v in range(8):
-            dense_ref[f * 64 + v * 8 : f * 64 + v * 8 + 8] = planes[v]
         for dim in (1, 2):
             for v, value in enumerate(turned(planes, dim, lane, row)):
                 at = dim * 320 + f * 64 + v * 8
@@ -260,18 +266,16 @@
     load_pick.wait()
     for g in range(6):
         side = g % 2
-        parts = three_parts(plane_rows(turns, g // 2, side, (g // 2) * 320))
+        parts = parts_of(2, plane_rows(turns, g // 2, side, (g // 2) * 320))
         rows = sum(dot(pick_ref[side], part) for part in parts)
-        for n, part in enumerate(three_parts(rows)):
+        for n, part in enumerate(parts_of(2, rows)):
             for kind in range(3):
                 left[kind, n, g * 32 : g * 32 + 32] = part[kind * 32 : kind * 32 + 32]
-    peak[1] = take_peaks(0, first)
-    second = send_peaks(1)
     load_tan.wait()
     for tile in range(6):
         kind = 0 if tile == 0 else 1 if tile < 5 else 2
         weights = tan_ref[:, tile * 256 : tile * 256 + 256]
-        out = sum(dot(left[kind, n], weights) for n in range(3))
+        out = sum(dot(left[kind, n], weights) for n in range(2))
         wide[2 * tile] = out[:, 0:128].reshape(12, 16, 128)
         if tile < 5:
             wide[2 * tile + 1] = out[:, 128:256].reshape(12, 16, 128)
@@ -304,9 +308,9 @@
         slab_copies.append(copy)
     for m in range(CAP):
         entry(REACH * CAP + m, got, REACH * CAP + m)
-    peak[2] = take_peaks(1, second)
-    third = send_peaks(2)
-    for c in want_copies + slab_copies:
+    peak[1] = take_peaks(0, first)
+    second = send_peaks(1)
+    for c in want_copies:
         c.wait_recv()
     second_block = [want_in[n] > 0.5 for n in range(2)]
     for n in range(2):
@@ -338,6 +342,10 @@
             )
     move_copies[0].start()
     move_copies[2].start()
+    peak[2] = take_peaks(1, second)
+    third = send_peaks(2)
+    for c in slab_copies:
+        c.wait_recv()
     for g in range(6):
         for qa in range(2):
             pair = []
@@ -356,9 +364,106 @@
                 stage_g[n, g, qa, 8:16] = jnp.where(pick, pair[1][1], pair[0][1])
     move_copies[1].start()
     move_copies[3].start()
-    top_ref[...] = take_peaks(2, third)
-    for c in move_copies:
-        c.wait_recv()
+    slots = []
+    for j in range(2):
+        source = mig_ref[j]
+        far = jnp.where(source // 2 < me, 2, 3)
+        slots.append(jnp.where(source // 2 == me, source % 2, far))
+    move_copies[0].wait_recv()
+    move_copies[2].wait_recv()
+    for f in range(5):
+        planes = []
+        for v in range(8):
+            own = turns[f * 64 + v * 8 : f * 64 + v * 8 + 8]
+            down, up = moved_ref[0, f, v // 2], moved_ref[1, f, v // 2]
+            for b in range(2):
+                away = 6 if b == 0 else 2
+                mine = jnp.where(slots[b] == b, own, pltpu.roll(own, away, 0))
+                other = jnp.where(slots[b] == 2, down, up)
+                if v % 2 != b:
+                    other = pltpu.roll(other, away, 0)
+                value = jnp.where(slots[b] < 2, mine, other)
+                both = value if b == 0 else jnp.where((row & 2) == 0, both, value)
+            planes.append(both)
+        for a in range(3):
+            layout = planes if a == 0 else turned(planes, a, lane, row)
+            up, down = (4, 4) if a == 0 else (1, 7)
+            for v in range(8):
+                cells[a, f, 3 + v] = layout[v]
+            for layer in range(3):
+                cells[a, f, 2 - layer] = pltpu.roll(layout[7 - layer], up, 0)
+                cells[a, f, 11 + layer] = pltpu.roll(layout[layer], down, 0)
+    top = take_peaks(2, third)
+    fastest = top[0:8]
+    step = 0.4 / top[8:16]
+
+    def flux(a, p, u):
+        inv = 1.0 / u[0]
+        v = [u[1 + i] * inv for i in range(3)]
+        kinetic = u[1] * v[0] + u[2] * v[1] + u[3] * v[2]
+        pressure = 0.4 * (u[4] - 0.5 * kinetic)
+        flow = [u[1 + a]] + [u[1 + i] * v[a] for i in range(3)] + [(u[4] + pressure) * v[a]]
+        flow[1 + a] = flow[1 + a] + pressure
+        for f in range(5):
+            plus[a, f, p] = 0.5 * (flow[f] + fastest * u[f])
+            minus[a, f, p] = 0.5 * (flow[f] - fastest * u[f])
+
+    for a in range(3):
+
+        def inner(p, carry):
+            flux(a, p, [cells[a, f, p] for f in range(5)])
+            return carry
+
+        lax.fori_loop(3, 11, inner, 0, unroll=2)
+    move_copies[1].wait_recv()
+    move_copies[3].wait_recv()
+    for b in range(2):
+        for g in range(6):
+            for h in range(2):
+                base = (g // 2) * 128 + row_of(g // 2, g % 2, b, h)
+                rims[pl.ds(base, 8, stride=8), :] = ghost_ref[slots[b], g, h, 0:8]
+                rims[pl.ds(base + 64, 8, stride=8), :] = ghost_ref[slots[b], g, h, 8:16]
+    factor = step * rims[120:128]
+    for a in range(3):
+        lower = (row & (4 if a == 0 else 1)) == 0
+        for layer in range(3):
+            rim = [rims[a * 128 + (f * 3 + layer) * 8 : a * 128 + (f * 3 + layer) * 8 + 8] for f in range(5)]
+            low, high = 2 - layer, 11 + layer
+            flux(a, low, [jnp.where(lower, rim[f], cells[a, f, low]) for f in range(5)])
+            flux(a, high, [jnp.where(lower, cells[a, f, high], rim[f]) for f in range(5)])
+
+        def field(f, carry):
+            hat = weno(plus[a, f], 2, False) + weno(minus[a, f], 3, True)
+            change[a, f] = hat[1:] - hat[:-1]
+            return carry
+
+        lax.fori_loop(0, 5, field, 0)
+    for f in range(5):
+        second_part = turned_back([change[1, f, v] for v in range(8)], 1, lane, row)
+        third_part = turned_back([change[2, f, v] for v in range(8)], 2, lane, row)
+        for v in range(8):
+            moved = change[0, f, v] + second_part[v] + third_part[v]
+            result[f * 64 + v * 8 : f * 64 + v * 8 + 8] = cells[0, f, 3 + v] - factor * moved
+    load_lane.wait()
+    load_line.wait()
+    halves = [plane_rows(result, 0, half) for half in range(2)]
+    cubes = jnp.concatenate(
+        [halves[half][n * 8 : n * 8 + 8] for n in range(10) for half in range(2)], 0
+    )
+    smooth = sum(dot(part, lane_ref[...]) for part in parts_of(3, cubes))
+    smooth = sum(dot(line_ref[...], part) for part in parts_of(3, smooth))
+    for b in range(2):
+        kept = jnp.where(flag_ref[b] == 1, smooth[b * 80 : b * 80 + 80], cubes[b * 80 : b * 80 + 80])
+        for f in range(5):
+            for half in range(2):
+                at = f * 16 + half * 8
+                for h in range(2):
+                    base = f * 64 + row_of(0, half, b, h)
+                    result[pl.ds(base, 8, stride=8), :] = kept[at : at + 8, h * 128 : h * 128 + 128]
+    for f in range(5):
+        for c in range(32):
+            at = f * 64 + (c // 2 % 8) * 8 + (c // 16) * 4 + c % 2
+            out_ref[f, :, c * 128 : c * 128 + 128] = result[pl.ds(at, 2, stride=2), :]
     for c in first + second + third + want_copies + slab_copies + move_copies:
         c.wait_send()
 
@@ -400,112 +505,6 @@
     return centre + share if sign > 0 else centre - share
 
 
-def update_kernel(
-    n_core, dense_ref, moved_ref, ghost_ref, top_ref, mig_ref, flag_ref, lane_hbm, line_hbm, out_ref,
-    cells, rims, plus, minus, change, result, lane_ref, line_ref, load_s,
-):
-    load_lane = pltpu.make_async_copy(lane_hbm, lane_ref, load_s.at[0])
-    load_line = pltpu.make_async_copy(line_hbm, line_ref, load_s.at[1])
-    load_lane.start()
-    load_line.start()
-    me = lax.axis_index("node") * n_core + lax.axis_index("cores")
-    lane, row = iotas()
-    slots = []
-    for j in range(2):
-        source = mig_ref[j]
-        far = jnp.where(source // 2 < me, 2, 3)
-        slots.append(jnp.where(source // 2 == me, source % 2, far))
-    for b in range(2):
-        for g in range(6):
-            for h in range(2):
-                base = (g // 2) * 128 + row_of(g // 2, g % 2, b, h)
-                rims[pl.ds(base, 8, stride=8), :] = ghost_ref[slots[b], g, h, 0:8]
-                rims[pl.ds(base + 64, 8, stride=8), :] = ghost_ref[slots[b], g, h, 8:16]
-    for f in range(5):
-        planes = []
-        for v in range(8):
-            own = dense_ref[f * 64 + v * 8 : f * 64 + v * 8 + 8]
-            down, up = moved_ref[0, f, v // 2], moved_ref[1, f, v // 2]
-            for b in range(2):
-                away = 6 if b == 0 else 2
-                mine = jnp.where(slots[b] == b, own, pltpu.roll(own, away, 0))
-                other = jnp.where(slots[b] == 2, down, up)
-                if v % 2 != b:
-                    other = pltpu.roll(other, away, 0)
-                value = jnp.where(slots[b] < 2, mine, other)
-                both = value if b == 0 else jnp.where((row & 2) == 0, both, value)
-            planes.append(both)
-        for a in range(3):
-            layout = planes if a == 0 else turned(planes, a, lane, row)
-            lower = (row & (4 if a == 0 else 1)) == 0
-            up, down = (4, 4) if a == 0 else (1, 7)
-            for v in range(8):
-                cells[a, f, 3 + v] = layout[v]
-            for layer in range(3):
-                rim = rims[a * 128 + (f * 3 + layer) * 8 : a * 128 + (f * 3 + layer) * 8 + 8]
-                cells[a, f, 2 - layer] = jnp.where(lower, rim, pltpu.roll(layout[7 - layer], up, 0))
-                cells[a, f, 11 + layer] = jnp.where(lower, pltpu.roll(layout[layer], down, 0), rim)
-    fastest = top_ref[0:8]
-    step = 0.4 / top_ref[8:16]
-    factor = step * rims[120:128]
-    for a in range(3):
-
-        def flux(p, carry):
-            u = [cells[a, f, p] for f in range(5)]
-            inv = 1.0 / u[0]
-            v = [u[1 + i] * inv for i in range(3)]
-            kinetic = u[1] * v[0] + u[2] * v[1] + u[3] * v[2]
-            pressure = 0.4 * (u[4] - 0.5 * kinetic)
-            flow = [u[1 + a]] + [u[1 + i] * v[a] for i in range(3)] + [(u[4] + pressure) * v[a]]
-            flow[1 + a] = flow[1 + a] + pressure
-            for f in range(5):
-                plus[f, p] = 0.5 * (flow[f] + fastest * u[f])
-                minus[f, p] = 0.5 * (flow[f] - fastest * u[f])
-            return carry
-
-        lax.fori_loop(0, 14, flux, 0, unroll=2)
-
-        def field(f, carry):
-            hat = weno(plus[f], 2, False) + weno(minus[f], 3, True)
-            change[a, f] = hat[1:] - hat[:-1]
-            return carry
-
-        lax.fori_loop(0, 5, field, 0)
-    for f in range(5):
-        second = turned_back([change[1, f, v] for v in range(8)], 1, lane, row)
-        third = turned_back([change[2, f, v] for v in range(8)], 2, lane, row)
-        for v in range(8):
-            moved = change[0, f, v] + second[v] + third[v]
-            result[f * 64 + v * 8 : f * 64 + v * 8 + 8] = cells[0, f, 3 + v] - factor * moved
-
-    load_lane.wait()
-    load_line.wait()
-
-    @pl.when(jnp.logical_or(flag_ref[0] == 1, flag_ref[1] == 1))
-    def _():
-        halves = [plane_rows(result, 0, half) for half in range(2)]
-        cubes = jnp.concatenate(
-            [halves[half][n * 8 : n * 8 + 8] for n in range(10) for half in range(2)], 0
-        )
-        smooth = sum(dot(part, lane_ref[...]) for part in three_parts(cubes))
-        smooth = sum(dot(line_ref[...], part) for part in three_parts(smooth))
-        for b in range(2):
-
-            @pl.when(flag_ref[b] == 1)
-            def _():
-                for f in range(5):
-                    for half in range(2):
-                        at = (b * 5 + f) * 16 + half * 8
-                        for h in range(2):
-                            base = f * 64 + row_of(0, half, b, h)
-                            result[pl.ds(base, 8, stride=8), :] = smooth[at : at + 8, h * 128 : h * 128 + 128]
-
-    for f in range(5):
-        for c in range(32):
-            at = f * 64 + (c // 2 % 8) * 8 + (c // 16) * 4 + c % 2
-            out_ref[f, :, c * 128 : c * 128 + 128] = result[pl.ds(at, 2, stride=2), :]
-
-
 def solution(mesh):
     n_node, n_core = mesh.shape["node"], mesh.shape["cores"]
     nz = max(1, int(round(n_node**0.5)))
@@ -516,19 +515,15 @@
     groups = n_core - 1 + nz - 1 + n_node // nz - 1
 
     def body(block_state, levels, send_table, receive_table, migration, coarsen_flags):
-        dense, ghosts, moved, top = pl.pallas_call(
-            functools.partial(exchange_kernel, nz, n_node, n_core),
-            out_shape=(
-                jax.ShapeDtypeStruct((320, 128), F32),
-                jax.ShapeDtypeStruct((4, 6, 2, 16, 128), F32),
-                jax.ShapeDtypeStruct((2, 5, 4, 8, 128), F32),
-                jax.ShapeDtypeStruct((16, 128), F32),
-            ),
-            in_specs=[VM, SM, SM, SM, SM, HB, HB],
-            out_specs=(VM, VM, VM, VM),
+        state = pl.pallas_call(
+            functools.partial(section_kernel, nz, n_node, n_core),
+            out_shape=jax.ShapeDtypeStruct((5, 2, 4096), F32),
+            in_specs=[HB, SM, SM, SM, SM, SM, HB, HB, HB, HB],
+            out_specs=VM,
             scratch_shapes=[
+                pltpu.VMEM((5, 2, 4096), F32),
                 pltpu.VMEM((960, 128), F32),
-                pltpu.VMEM((3, 3, 192, 256), BF16),
+                pltpu.VMEM((3, 2, 192, 256), BF16),
                 pltpu.VMEM((11, 12, 16, 128), F32),
                 pltpu.VMEM((SLOTS - CAP, 8, 128), F32),
                 pltpu.VMEM((SLOTS, 8, 128), F32),
@@ -536,10 +531,20 @@
                 pltpu.VMEM((2, 8, 128), F32),
                 pltpu.VMEM((2, 6, 2, 16, 128), F32),
                 pltpu.VMEM((2, 5, 4, 8, 128), F32),
+                pltpu.VMEM((4, 6, 2, 16, 128), F32),
+                pltpu.VMEM((2, 5, 4, 8, 128), F32),
                 pltpu.VMEM((3, 16, 128), F32),
                 pltpu.VMEM((groups, 16, 128), F32),
+                pltpu.VMEM((3, 5, 14, 8, 128), F32),
+                pltpu.VMEM((3 * 16 * 8, 128), F32),
+                pltpu.VMEM((3, 5, 14, 8, 128), F32),
+                pltpu.VMEM((3, 5, 14, 8, 128), F32),
+                pltpu.VMEM((3, 5, 8, 8, 128), F32),
+                pltpu.VMEM((320, 128), F32),
                 pltpu.VMEM((256, 1536), BF16),
                 pltpu.VMEM((2, 96, 80), BF16),
+                pltpu.VMEM((256, 256), BF16),
+                pltpu.VMEM((160, 160), BF16),
                 pltpu.SemaphoreType.DMA((6,)),
                 pltpu.SemaphoreType.DMA((6,)),
                 pltpu.SemaphoreType.DMA((2,)),
@@ -548,36 +553,15 @@
                 pltpu.SemaphoreType.DMA((4,)),
                 pltpu.SemaphoreType.DMA((groups,)),
                 pltpu.SemaphoreType.DMA((groups,)),
-                pltpu.SemaphoreType.DMA((2,)),
+                pltpu.SemaphoreType.DMA((5,)),
             ],
             compiler_params=pltpu.CompilerParams(
-                collective_id=0, has_side_effects=True, vmem_limit_bytes=48 << 20
+                collective_id=0, has_side_effects=True, vmem_limit_bytes=VMEM_BYTES
             ),
-            name="exchange",
+            name="section",
         )(
-            jnp.transpose(block_state, (1, 0, 2)), send_table, receive_table, migration, levels,
+            jnp.transpose(block_state, (1, 0, 2)), send_table, receive_table, migration, levels, coarsen_flags,
             jnp.asarray(tangents, BF16), jnp.asarray(picks, BF16),
-        )
-        state = pl.pallas_call(
-            functools.partial(update_kernel, n_core),
-            out_shape=jax.ShapeDtypeStruct((5, 2, 4096), F32),
-            in_specs=[VM, VM, VM, VM, SM, SM, HB, HB],
-            out_specs=VM,
-            scratch_shapes=[
-                pltpu.VMEM((3, 5, 14, 8, 128), F32),
-                pltpu.VMEM((3 * 16 * 8, 128), F32),
-                pltpu.VMEM((5, 14, 8, 128), F32),
-                pltpu.VMEM((5, 14, 8, 128), F32),
-                pltpu.VMEM((3, 5, 8, 8, 128), F32),
-                pltpu.VMEM((320, 128), F32),
-                pltpu.VMEM((256, 256), BF16),
-                pltpu.VMEM((160, 160), BF16),
-                pltpu.SemaphoreType.DMA((2,)),
-            ],
-            compiler_params=pltpu.CompilerParams(vmem_limit_bytes=48 << 20),
-            name="update",
-        )(
-            dense, moved, ghosts, top, migration, coarsen_flags,
             jnp.asarray(lane_smoother, BF16), jnp.asarray(line_smoother, BF16),
         )
         return jnp.transpose(state, (1, 0, 2))

time: 43 us -> 35.2 us (0.82)
  Pallas kernels: 37.8 us -> 33.4 us
  local copies, waits for them, and re-layouts: 4.85 us -> 1.59 us
    pallas_call x2 -> x1, Pallas kernels: 37.8 us -> 33.4 us  [body(): pl.pallas_call(functools.partial(section_kernel, nz, n_node, n_core), out...]
    unnamed x20 -> x1, local copies, waits for them, and re-layouts: 4.85 us -> 1.59 us
where the time goes in v2:
time: 35.2 us; the launch traced here: 35 us
  Pallas kernels  33.4 us (95%)
  local copies, waits for them, and re-layouts  1.59 us (5%)
    pallas_call x1, Pallas kernels, body(): pl.pallas_call(functools.partial(section_kernel, nz, n_node, n_core), out...  33.4 us
    unnamed x1, local copies, waits for them, and re-layouts  1.59 us

profile of v2, /device:TPU:1, one launch (start us, length us, event | category | flops | bytes accessed | tf_op | source)
XLA Modules:
  0.0 35.0 jit_solution(9113427361287668814)
XLA Ops:
  0.0 33.4 %section.1 = f32[5,2,4096]{2,1,0:T(2,128)} custom-call(f32[5,2,4096]{2,1,0:T(2,128)} %bitcast.3, s32[5,49]{1,0:T(8,128)} %send_ref.1, s32[48]{0:T(128)} %recv_ref.1, s32[2]{0:T(128)} %mig_ref.1, s32[2]{0:T(128)} %level_ref.1, s32[2]{0:T(128)} %flag_ref.1, bf16[256,1536]{1,0:T(8,128)(2,1)} %constant.8.clone.tan_hbm, ...), custom_call_target="tpu_custom_call" | custom-call | tf_op jit(solution)/shard_map/section/pallas_call | solution.py:518
  33.4 1.6 %copy.12 = f32[2,5,4096]{2,0,1:T(2,128)} copy(f32[2,5,4096]{2,0,1:T(2,128)} %bitcast.2) | data formatting | bytes 327680

commit v3 on v2

--- a/solution.py
+++ b/solution.py
@@ -96,6 +96,11 @@
     return lane, row
 
 
+def inverse(x):
+    guess = pl.reciprocal(x, approx=True)
+    return guess * (2.0 - x * guess)
+
+
 def swap(planes, lane, bit, reach):
     keep = (lane & reach) == 0
     out = list(planes)
@@ -156,10 +161,11 @@
 
 def section_kernel(
     nz, n_node, n_core,
-    x_hbm, send_ref, recv_ref, mig_ref, level_ref, flag_ref, tan_hbm, pick_hbm, lane_hbm, line_hbm,
+    x_hbm, send_hbm, recv_hbm, mig_hbm, level_hbm, flag_hbm, tan_hbm, pick_hbm, lane_hbm, line_hbm,
     out_ref,
-    x_ref, turns, left, wide, slabs, got, want_out, want_in, stage_g, stage_x, ghost_ref, moved_ref, peak, peaks,
-    cells, rims, plus, minus, change, result, tan_ref, pick_ref, lane_ref, line_ref,
+    x_ref, turns, left, wide, slabs, got, want_out, want_in, stage_g, stage_x, ghosts, moved_ref, peak, peaks,
+    cells, rims, flows, change, result, tan_ref, pick_ref, lane_ref, line_ref,
+    send_ref, recv_ref, mig_ref, level_ref, flag_ref,
     slab_s, slab_r, want_s, want_r, move_s, move_r, peak_s, peak_r, load_s,
 ):
     node, core = lax.axis_index("node"), lax.axis_index("cores")
@@ -173,48 +179,68 @@
         other = (me + offset + total) % total
         return (other // n_core, other % n_core)
 
+    def around(count):
+        return sorted(range(1, count), key=lambda t: (-min(t, count - t), t))
+
     groups = [
-        [(node, (core + t) % n_core) for t in range(1, n_core)],
-        [(y * nz + (z + t) % nz, core) for t in range(1, nz)],
-        [(((y + t) % ny) * nz + z, core) for t in range(1, ny)],
+        [(node, (core + t) % n_core) for t in around(n_core)],
+        [(y * nz + (z + t) % nz, core) for t in around(nz)],
+        [(((y + t) % ny) * nz + z, core) for t in around(ny)],
     ]
     offsets = [o for o in range(-REACH, REACH + 1) if o != 0]
     partners = [d for group in groups for d in group] + [along(o) for o in offsets]
     barrier = pltpu.get_barrier_semaphore()
     for d in partners:
         pl.semaphore_signal(barrier, inc=1, device_id=d, device_id_type=MESH)
-    load_x = pltpu.make_async_copy(x_hbm, x_ref, load_s.at[0])
-    load_pick = pltpu.make_async_copy(pick_hbm, pick_ref, load_s.at[1])
-    load_tan = pltpu.make_async_copy(tan_hbm, tan_ref, load_s.at[2])
-    load_lane = pltpu.make_async_copy(lane_hbm, lane_ref, load_s.at[3])
-    load_line = pltpu.make_async_copy(line_hbm, line_ref, load_s.at[4])
-    for load in (load_x, load_pick, load_tan, load_lane, load_line):
+    (load_x, load_level, load_mig, load_pick, load_send, load_tan, load_recv, load_flag, load_lane, load_line) = loads = [
+        pltpu.make_async_copy(source, target, load_s.at[n])
+        for n, (source, target) in enumerate(
+            (
+                (x_hbm, x_ref),
+                (level_hbm, level_ref),
+                (mig_hbm, mig_ref),
+                (pick_hbm, pick_ref),
+                (send_hbm, send_ref),
+                (tan_hbm, tan_ref),
+                (recv_hbm, recv_ref),
+                (flag_hbm, flag_ref),
+                (lane_hbm, lane_ref),
+                (line_hbm, line_ref),
+            )
+        )
+    ]
+    for load in loads:
         load.start()
 
+    firsts = [sum(len(g) for g in groups[:phase]) for phase in range(4)]
+
     def send_peaks(phase):
-        base = sum(len(g) for g in groups[:phase])
-        copies = [
+        for t, d in enumerate(groups[phase]):
             pltpu.make_async_remote_copy(
                 src_ref=peak.at[phase],
-                dst_ref=peaks.at[base + t],
-                send_sem=peak_s.at[base + t],
-                recv_sem=peak_r.at[base + t],
+                dst_ref=peaks.at[firsts[phase] + t],
+                send_sem=peak_s.at[phase],
+                recv_sem=peak_r.at[phase],
                 device_id=d,
                 device_id_type=MESH,
-            )
-            for t, d in enumerate(groups[phase])
-        ]
-        for c in copies:
-            c.start()
-        return copies
-
-    def take_peaks(phase, copies):
-        base = sum(len(g) for g in groups[:phase])
-        for c in copies:
-            c.wait_recv()
+            ).start()
+
+    def all_peaks(phase):
+        slots = peaks.at[pl.ds(firsts[phase], len(groups[phase]))]
+        return pltpu.make_async_remote_copy(
+            src_ref=slots,
+            dst_ref=slots,
+            send_sem=peak_s.at[phase],
+            recv_sem=peak_r.at[phase],
+            device_id=groups[phase][0],
+            device_id_type=MESH,
+        )
+
+    def take_peaks(phase):
+        all_peaks(phase).wait_recv()
         best = peak[phase]
-        for t in range(len(copies)):
-            best = jnp.maximum(best, peaks[base + t])
+        for t in range(len(groups[phase])):
+            best = jnp.maximum(best, peaks[firsts[phase] + t])
         return best
 
     load_x.wait()
@@ -225,17 +251,19 @@
     top = None
     for v in range(8):
         u = [turns[f * 64 + v * 8 : f * 64 + v * 8 + 8] for f in range(5)]
-        inv = 1.0 / u[0]
+        inv = inverse(u[0])
         vel = [u[1 + i] * inv for i in range(3)]
         kinetic = u[1] * vel[0] + u[2] * vel[1] + u[3] * vel[2]
         pressure = 0.4 * (u[4] - 0.5 * kinetic)
         speed = jnp.maximum(jnp.maximum(jnp.abs(vel[0]), jnp.abs(vel[1])), jnp.abs(vel[2]))
         speed = speed + jnp.sqrt(1.4 * pressure * inv)
         top = speed if v == 0 else jnp.maximum(top, speed)
+    load_level.wait()
+    load_mig.wait()
     scales = [lax.shift_left(jnp.int32(EDGE), level_ref[b]).astype(F32) for b in range(2)]
     rated = top * jnp.where((row & 2) == 0, scales[0], scales[1])
-    peak[0, 0:8] = jnp.full((8, 128), jnp.max(top), F32)
-    peak[0, 8:16] = jnp.full((8, 128), jnp.max(rated), F32)
+    upper = (lane[0:1] & 64) != 0
+    peak[0] = jnp.where(upper, jnp.max(rated), jnp.max(top))
     for n, direction in enumerate((1, -1)):
         want = jnp.int32(0)
         for j in range(2):
@@ -243,7 +271,7 @@
             want = want + jnp.where(source // 2 == me + direction, source % 2, 0)
         want_out[n] = jnp.full((8, 128), want, jnp.int32).astype(F32)
     pl.semaphore_wait(barrier, len(partners))
-    first = send_peaks(0)
+    send_peaks(0)
     want_copies = [
         pltpu.make_async_remote_copy(
             src_ref=want_out.at[n],
@@ -280,6 +308,7 @@
         if tile < 5:
             wide[2 * tile + 1] = out[:, 128:256].reshape(12, 16, 128)
     even = (lane & 8) == 0
+    load_send.wait()
 
     def entry(k, into, at):
         blk, g, kind = send_ref[0, k], send_ref[1, k], send_ref[2, k]
@@ -308,8 +337,12 @@
         slab_copies.append(copy)
     for m in range(CAP):
         entry(REACH * CAP + m, got, REACH * CAP + m)
-    peak[1] = take_peaks(0, first)
-    second = send_peaks(1)
+    load_recv.wait()
+    load_flag.wait()
+    peak[1] = take_peaks(0)
+    send_peaks(1)
+    peak[2] = take_peaks(1)
+    send_peaks(2)
     for c in want_copies:
         c.wait_recv()
     second_block = [want_in[n] > 0.5 for n in range(2)]
@@ -322,55 +355,48 @@
                 one = jnp.where(pick, pltpu.roll(one, 6, 0), one)
                 two = jnp.where(pick, two, pltpu.roll(two, 2, 0))
                 stage_x[n, f, t] = jnp.where((row & 2) == 0, one, two)
-    move_copies = []
-    for n, direction in enumerate((-1, 1)):
-        for m, (src, dst) in enumerate(
-            (
-                (stage_x.at[n], moved_ref.at[1 - n]),
-                (stage_g.at[n], ghost_ref.at[3 - n]),
-            )
-        ):
-            move_copies.append(
-                pltpu.make_async_remote_copy(
-                    src_ref=src,
-                    dst_ref=dst,
-                    send_sem=move_s.at[2 * n + m],
-                    recv_sem=move_r.at[2 * n + m],
-                    device_id=along(direction),
-                    device_id_type=MESH,
-                )
-            )
-    move_copies[0].start()
-    move_copies[2].start()
-    peak[2] = take_peaks(1, second)
-    third = send_peaks(2)
+    def move(n, piece, source, target):
+        copy = pltpu.make_async_remote_copy(
+            src_ref=source,
+            dst_ref=target,
+            send_sem=move_s.at[n, piece],
+            recv_sem=move_r.at[n, piece],
+            device_id=along((-1, 1)[n]),
+            device_id_type=MESH,
+        )
+        copy.start()
+        return copy
+
+    state_copies = [move(n, 3, stage_x.at[n], moved_ref.at[1 - n]) for n in range(2)]
     for c in slab_copies:
         c.wait_recv()
-    for g in range(6):
-        for qa in range(2):
-            pair = []
-            for b in range(2):
-                at = (b * 6 + g) * 4 + 2 * qa
-                one, two = got[recv_ref[at]], got[recv_ref[at + 1]]
-                low = jnp.where(even, one, pltpu.roll(two, 8, 1))
-                high = jnp.where(even, pltpu.roll(one, 120, 1), two)
-                high = jnp.where(row == 7, scales[b], high)
-                ghost_ref[b, g, qa, 0:8] = low
-                ghost_ref[b, g, qa, 8:16] = high
-                pair.append((low, high))
-            for n in range(2):
-                pick = second_block[n]
-                stage_g[n, g, qa, 0:8] = jnp.where(pick, pair[1][0], pair[0][0])
-                stage_g[n, g, qa, 8:16] = jnp.where(pick, pair[1][1], pair[0][1])
-    move_copies[1].start()
-    move_copies[3].start()
+    rim_copies = []
+    for a in range(3):
+        for side in range(2):
+            g = 2 * a + side
+            for qa in range(2):
+                pair = []
+                for b in range(2):
+                    at = (b * 6 + g) * 4 + 2 * qa
+                    one, two = got[recv_ref[at]], got[recv_ref[at + 1]]
+                    low = jnp.where(even, one, pltpu.roll(two, 8, 1))
+                    high = jnp.where(even, pltpu.roll(one, 120, 1), two)
+                    high = jnp.where(row == 7, scales[b], high)
+                    ghosts[a][b, side, qa, 0:8] = low
+                    ghosts[a][b, side, qa, 8:16] = high
+                    pair.append((low, high))
+                for n in range(2):
+                    pick = second_block[n]
+                    stage_g[a, n, side, qa, 0:8] = jnp.where(pick, pair[1][0], pair[0][0])
+                    stage_g[a, n, side, qa, 8:16] = jnp.where(pick, pair[1][1], pair[0][1])
+        rim_copies.append([move(n, a, stage_g.at[a, n], ghosts[a].at[3 - n]) for n in range(2)])
     slots = []
     for j in range(2):
         source = mig_ref[j]
         far = jnp.where(source // 2 < me, 2, 3)
         slots.append(jnp.where(source // 2 == me, source % 2, far))
-    move_copies[0].wait_recv()
-    move_copies[2].wait_recv()
+    for c in state_copies:
+        c.wait_recv()
     for f in range(5):
         planes = []
         for v in range(8):
@@ -393,20 +419,15 @@
             for layer in range(3):
                 cells[a, f, 2 - layer] = pltpu.roll(layout[7 - layer], up, 0)
                 cells[a, f, 11 + layer] = pltpu.roll(layout[layer], down, 0)
-    top = take_peaks(2, third)
-    fastest = top[0:8]
-    step = 0.4 / top[8:16]
-
     def flux(a, p, u):
-        inv = 1.0 / u[0]
+        inv = inverse(u[0])
         v = [u[1 + i] * inv for i in range(3)]
         kinetic = u[1] * v[0] + u[2] * v[1] + u[3] * v[2]
         pressure = 0.4 * (u[4] - 0.5 * kinetic)
         flow = [u[1 + a]] + [u[1 + i] * v[a] for i in range(3)] + [(u[4] + pressure) * v[a]]
         flow[1 + a] = flow[1 + a] + pressure
         for f in range(5):
-            plus[a, f, p] = 0.5 * (flow[f] + fastest * u[f])
-            minus[a, f, p] = 0.5 * (flow[f] - fastest * u[f])
+            flows[a, f, p] = 0.5 * flow[f]
 
     for a in range(3):
 
@@ -414,26 +435,36 @@
             flux(a, p, [cells[a, f, p] for f in range(5)])
             return carry
 
-        lax.fori_loop(3, 11, inner, 0, unroll=2)
-    move_copies[1].wait_recv()
-    move_copies[3].wait_recv()
-    for b in range(2):
-        for g in range(6):
-            for h in range(2):
-                base = (g // 2) * 128 + row_of(g // 2, g % 2, b, h)
-                rims[pl.ds(base, 8, stride=8), :] = ghost_ref[slots[b], g, h, 0:8]
-                rims[pl.ds(base + 64, 8, stride=8), :] = ghost_ref[slots[b], g, h, 8:16]
-    factor = step * rims[120:128]
+        lax.fori_loop(3, 11, inner, 0, unroll=4)
+    top = take_peaks(2)
+    half_fastest = 0.5 * jnp.max(jnp.where(upper, 0.0, top))
+    step = 0.4 / jnp.full((8, 128), jnp.max(jnp.where(upper, top, 0.0)), F32)
     for a in range(3):
+        for c in rim_copies[a]:
+            c.wait_recv()
+        for b in range(2):
+            for side in range(2):
+                for h in range(2):
+                    base = a * 128 + row_of(a, side, b, h)
+                    rims[pl.ds(base, 8, stride=8), :] = ghosts[a][slots[b], side, h, 0:8]
+                    rims[pl.ds(base + 64, 8, stride=8), :] = ghosts[a][slots[b], side, h, 8:16]
+        if a == 0:
+            factor = step * rims[120:128]
         lower = (row & (4 if a == 0 else 1)) == 0
         for layer in range(3):
             rim = [rims[a * 128 + (f * 3 + layer) * 8 : a * 128 + (f * 3 + layer) * 8 + 8] for f in range(5)]
             low, high = 2 - layer, 11 + layer
-            flux(a, low, [jnp.where(lower, rim[f], cells[a, f, low]) for f in range(5)])
-            flux(a, high, [jnp.where(lower, cells[a, f, high], rim[f]) for f in range(5)])
+            below = [jnp.where(lower, rim[f], cells[a, f, low]) for f in range(5)]
+            above = [jnp.where(lower, cells[a, f, high], rim[f]) for f in range(5)]
+            for f in range(5):
+                cells[a, f, low] = below[f]
+                cells[a, f, high] = above[f]
+            flux(a, low, below)
+            flux(a, high, above)
 
         def field(f, carry):
-            hat = weno(plus[a, f], 2, False) + weno(minus[a, f], 3, True)
+            flow, spread = flows[a, f], half_fastest * cells[a, f]
+            hat = weno(flow + spread, 2, False) + weno(flow - spread, 3, True)
             change[a, f] = hat[1:] - hat[:-1]
             return carry
 
@@ -464,7 +495,9 @@
         for c in range(32):
             at = f * 64 + (c // 2 % 8) * 8 + (c // 16) * 4 + c % 2
             out_ref[f, :, c * 128 : c * 128 + 128] = result[pl.ds(at, 2, stride=2), :]
-    for c in first + second + third + want_copies + slab_copies + move_copies:
+    for phase in range(3):
+        all_peaks(phase).wait_send()
+    for c in want_copies + slab_copies + state_copies + [c for pair in rim_copies for c in pair]:
         c.wait_send()
 
 
@@ -518,7 +551,7 @@
         state = pl.pallas_call(
             functools.partial(section_kernel, nz, n_node, n_core),
             out_shape=jax.ShapeDtypeStruct((5, 2, 4096), F32),
-            in_specs=[HB, SM, SM, SM, SM, SM, HB, HB, HB, HB],
+            in_specs=[HB] * 10,
             out_specs=VM,
             scratch_shapes=[
                 pltpu.VMEM((5, 2, 4096), F32),
@@ -529,15 +562,14 @@
                 pltpu.VMEM((SLOTS, 8, 128), F32),
                 pltpu.VMEM((2, 8, 128), F32),
                 pltpu.VMEM((2, 8, 128), F32),
-                pltpu.VMEM((2, 6, 2, 16, 128), F32),
+                pltpu.VMEM((3, 2, 2, 2, 16, 128), F32),
                 pltpu.VMEM((2, 5, 4, 8, 128), F32),
-                pltpu.VMEM((4, 6, 2, 16, 128), F32),
+                [pltpu.VMEM((4, 2, 2, 16, 128), F32)] * 3,
                 pltpu.VMEM((2, 5, 4, 8, 128), F32),
-                pltpu.VMEM((3, 16, 128), F32),
-                pltpu.VMEM((groups, 16, 128), F32),
+                pltpu.VMEM((3, 1, 128), F32),
+                pltpu.VMEM((groups, 1, 128), F32),
                 pltpu.VMEM((3, 5, 14, 8, 128), F32),
                 pltpu.VMEM((3 * 16 * 8, 128), F32),
-                pltpu.VMEM((3, 5, 14, 8, 128), F32),
                 pltpu.VMEM((3, 5, 14, 8, 128), F32),
                 pltpu.VMEM((3, 5, 8, 8, 128), F32),
                 pltpu.VMEM((320, 128), F32),
@@ -545,15 +577,20 @@
                 pltpu.VMEM((2, 96, 80), BF16),
                 pltpu.VMEM((256, 256), BF16),
                 pltpu.VMEM((160, 160), BF16),
+                pltpu.SMEM((5, SLOTS), jnp.int32),
+                pltpu.SMEM((48,), jnp.int32),
+                pltpu.SMEM((2,), jnp.int32),
+                pltpu.SMEM((2,), jnp.int32),
+                pltpu.SMEM((2,), jnp.int32),
                 pltpu.SemaphoreType.DMA((6,)),
                 pltpu.SemaphoreType.DMA((6,)),
                 pltpu.SemaphoreType.DMA((2,)),
                 pltpu.SemaphoreType.DMA((2,)),
-                pltpu.SemaphoreType.DMA((4,)),
-                pltpu.SemaphoreType.DMA((4,)),
-                pltpu.SemaphoreType.DMA((groups,)),
-                pltpu.SemaphoreType.DMA((groups,)),
-                pltpu.SemaphoreType.DMA((5,)),
+                pltpu.SemaphoreType.DMA((2, 4)),
+                pltpu.SemaphoreType.DMA((2, 4)),
+                pltpu.SemaphoreType.DMA((3,)),
+                pltpu.SemaphoreType.DMA((3,)),
+                pltpu.SemaphoreType.DMA((10,)),
             ],
             compiler_params=pltpu.CompilerParams(
                 collective_id=0, has_side_effects=True, vmem_limit_bytes=VMEM_BYTES

time: 35.2 us -> 33.8 us (0.960)
  Pallas kernels: 33.4 us -> 32 us
    pallas_call x1, Pallas kernels: 33.4 us -> 32 us  [body(): pl.pallas_call(functools.partial(section_kernel, nz, n_node, n_core), out...]
where the time goes in v3:
time: 33.8 us; the launch traced here: 33.6 us
  Pallas kernels  32 us (95%)
  local copies, waits for them, and re-layouts  1.59 us (5%)
    pallas_call x1, Pallas kernels, body(): pl.pallas_call(functools.partial(section_kernel, nz, n_node, n_core), out...  32 us
    unnamed x1, local copies, waits for them, and re-layouts  1.59 us

profile of v3, /device:TPU:1, one launch (start us, length us, event | category | flops | bytes accessed | tf_op | source)
XLA Modules:
  0.0 33.6 jit_solution(17597081181249417444)
XLA Ops:
  0.0 32.0 %section.1 = f32[5,2,4096]{2,1,0:T(2,128)} custom-call(f32[5,2,4096]{2,1,0:T(2,128)} %bitcast.3, s32[5,49]{1,0:T(8,128)} %send_hbm.1, s32[48]{0:T(128)} %recv_hbm.1, s32[2]{0:T(128)} %mig_hbm.1, s32[2]{0:T(128)} %level_hbm.1, s32[2]{0:T(128)} %flag_hbm.1, bf16[256,1536]{1,0:T(8,128)(2,1)} %constant.8.clone.tan_hbm, ...), custom_call_target="tpu_custom_call" | custom-call | tf_op jit(solution)/shard_map/section/pallas_call | solution.py:551
  32.0 1.6 %copy.12 = f32[2,5,4096]{2,0,1:T(2,128)} copy(f32[2,5,4096]{2,0,1:T(2,128)} %bitcast.2) | data formatting | bytes 327680

commit v4 on v3

--- a/solution.py
+++ b/solution.py
@@ -187,7 +187,7 @@
         [(y * nz + (z + t) % nz, core) for t in around(nz)],
         [(((y + t) % ny) * nz + z, core) for t in around(ny)],
     ]
-    offsets = [o for o in range(-REACH, REACH + 1) if o != 0]
+    offsets = [side * o for o in range(REACH, 0, -1) for side in (-1, 1)]
     partners = [d for group in groups for d in group] + [along(o) for o in offsets]
     barrier = pltpu.get_barrier_semaphore()
     for d in partners:
@@ -341,8 +341,6 @@
     load_flag.wait()
     peak[1] = take_peaks(0)
     send_peaks(1)
-    peak[2] = take_peaks(1)
-    send_peaks(2)
     for c in want_copies:
         c.wait_recv()
     second_block = [want_in[n] > 0.5 for n in range(2)]
@@ -368,6 +366,8 @@
         return copy
 
     state_copies = [move(n, 3, stage_x.at[n], moved_ref.at[1 - n]) for n in range(2)]
+    peak[2] = take_peaks(1)
+    send_peaks(2)
     for c in slab_copies:
         c.wait_recv()
     rim_copies = []
@@ -481,8 +481,8 @@
     cubes = jnp.concatenate(
         [halves[half][n * 8 : n * 8 + 8] for n in range(10) for half in range(2)], 0
     )
-    smooth = sum(dot(part, lane_ref[...]) for part in parts_of(3, cubes))
-    smooth = sum(dot(line_ref[...], part) for part in parts_of(3, smooth))
+    smooth = sum(dot(part, lane_ref[...]) for part in parts_of(2, cubes))
+    smooth = sum(dot(line_ref[...], part) for part in parts_of(2, smooth))
     for b in range(2):
         kept = jnp.where(flag_ref[b] == 1, smooth[b * 80 : b * 80 + 80], cubes[b * 80 : b * 80 + 80])
         for f in range(5):

time: 33.8 us -> 32.8 us (0.970)
  Pallas kernels: 32 us -> 31.1 us
    pallas_call x1, Pallas kernels: 32 us -> 31.1 us  [body(): pl.pallas_call(functools.partial(section_kernel, nz, n_node, n_core), out...]
where the time goes in v4:
time: 32.8 us; the launch traced here: 32.7 us
  Pallas kernels  31.1 us (95%)
  local copies, waits for them, and re-layouts  1.59 us (5%)
    pallas_call x1, Pallas kernels, body(): pl.pallas_call(functools.partial(section_kernel, nz, n_node, n_core), out...  31.1 us
    unnamed x1, local copies, waits for them, and re-layouts  1.59 us

profile of v4, /device:TPU:1, one launch (start us, length us, event | category | flops | bytes accessed | tf_op | source)
XLA Modules:
  0.0 32.7 jit_solution(538061234071353641)
XLA Ops:
  0.0 31.1 %section.1 = f32[5,2,4096]{2,1,0:T(2,128)} custom-call(f32[5,2,4096]{2,1,0:T(2,128)} %bitcast.3, s32[5,49]{1,0:T(8,128)} %send_hbm.1, s32[48]{0:T(128)} %recv_hbm.1, s32[2]{0:T(128)} %mig_hbm.1, s32[2]{0:T(128)} %level_hbm.1, s32[2]{0:T(128)} %flag_hbm.1, bf16[256,1536]{1,0:T(8,128)(2,1)} %constant.8.clone.tan_hbm, ...), custom_call_target="tpu_custom_call" | custom-call | tf_op jit(solution)/shard_map/section/pallas_call | solution.py:551
  31.1 1.6 %copy.12 = f32[2,5,4096]{2,0,1:T(2,128)} copy(f32[2,5,4096]{2,0,1:T(2,128)} %bitcast.2) | data formatting | bytes 327680

commit v5 on v4

--- a/solution.py
+++ b/solution.py
@@ -435,10 +435,11 @@
             flux(a, p, [cells[a, f, p] for f in range(5)])
             return carry
 
-        lax.fori_loop(3, 11, inner, 0, unroll=4)
-    top = take_peaks(2)
-    half_fastest = 0.5 * jnp.max(jnp.where(upper, 0.0, top))
-    step = 0.4 / jnp.full((8, 128), jnp.max(jnp.where(upper, top, 0.0)), F32)
+        lax.fori_loop(3, 11, inner, 0, unroll=8)
+    top = jnp.broadcast_to(take_peaks(2), (8, 128))
+    other_half = pltpu.roll(top, 64, 1)
+    half_fastest = 0.5 * jnp.where((lane & 64) != 0, other_half, top)
+    step = 0.4 / jnp.where((lane & 64) != 0, top, other_half)
     for a in range(3):
         for c in rim_copies[a]:
             c.wait_recv()
@@ -468,7 +469,7 @@
             change[a, f] = hat[1:] - hat[:-1]
             return carry
 
-        lax.fori_loop(0, 5, field, 0)
+        lax.fori_loop(0, 5, field, 0, unroll=5)
     for f in range(5):
         second_part = turned_back([change[1, f, v] for v in range(8)], 1, lane, row)
         third_part = turned_back([change[2, f, v] for v in range(8)], 2, lane, row)

time: 32.8 us -> 32.1 us (0.979)
  Pallas kernels: 31.1 us -> 30.4 us
    pallas_call x1, Pallas kernels: 31.1 us -> 30.4 us  [body(): pl.pallas_call(functools.partial(section_kernel, nz, n_node, n_core), out...]
where the time goes in v5:
time: 32.1 us; the launch traced here: 32 us
  Pallas kernels  30.4 us (95%)
  local copies, waits for them, and re-layouts  1.59 us (5%)
    pallas_call x1, Pallas kernels, body(): pl.pallas_call(functools.partial(section_kernel, nz, n_node, n_core), out...  30.4 us
    unnamed x1, local copies, waits for them, and re-layouts  1.59 us

profile of v5, /device:TPU:1, one launch (start us, length us, event | category | flops | bytes accessed | tf_op | source)
XLA Modules:
  0.0 32.0 jit_solution(15202707088660741311)
XLA Ops:
  0.0 30.4 %section.1 = f32[5,2,4096]{2,1,0:T(2,128)} custom-call(f32[5,2,4096]{2,1,0:T(2,128)} %bitcast.3, s32[5,49]{1,0:T(8,128)} %send_hbm.1, s32[48]{0:T(128)} %recv_hbm.1, s32[2]{0:T(128)} %mig_hbm.1, s32[2]{0:T(128)} %level_hbm.1, s32[2]{0:T(128)} %flag_hbm.1, bf16[256,1536]{1,0:T(8,128)(2,1)} %constant.8.clone.tan_hbm, ...), custom_call_target="tpu_custom_call" | custom-call | tf_op jit(solution)/shard_map/section/pallas_call | solution.py:552
  30.4 1.6 %copy.12 = f32[2,5,4096]{2,0,1:T(2,128)} copy(f32[2,5,4096]{2,0,1:T(2,128)} %bitcast.2) | data formatting | bytes 327680
